TPU v7x, 32 devices: a whole 2x2x4 slice. The times are simulated.
32 devices in a mesh: gx: 4 (over y, x), yz: 8 (over z, core).
Axes of the slice: x: 2, y: 2, z: 4, core: 2. Of those that a mesh axis runs over, the one named last changes fastest.
Arguments:
- spin_vectors: float32 [3, 2, 16, 16, 128], P(None, None, 'gx', 'yz'), may hold values from -1 to 1, as said below
- pair_weight: float32 [112, 128], replicated, may hold values from -0.5 to 0.5
- mix_weight: float32 [128, 128], replicated, may hold values from -0.5 to 0.5
- mix_bias: float32 [128], replicated, may hold values from -3 to 3
- out_weight: float32 [128], replicated, may hold values from -0.5 to 0.5
Outputs:
- spins_next: float32 [3, 2, 16, 16, 128], P(None, None, 'gx', 'yz')
- field_next: float32 [3, 2, 16, 16, 128], P(None, None, 'gx', 'yz')
Inputs may be any that keep to these rules, and one draw needn't show every extreme that they name: `spin_vectors`: every atom's spin has unit length.
All inputs are finite; a program needn't handle non-finite values.
Results may differ from a plain program's by a relative error of at most 0.0003.
Values sent between devices are 32-bit elements; how exact they have to be, the bound alone decides.
No kernel may reach another device: no remote copies, remote signals or barrier semaphores. Data moves between devices by JAX's collectives and lax.ppermute only.
A program may use at most 128 MiB of HBM per device.

v0:
```python
import functools

import jax
import jax.numpy as jnp
from jax import lax
from jax.experimental import pallas as pl
from jax.experimental.pallas import tpu as pltpu
from jax.sharding import PartitionSpec as P

NB = 8
TIME_STEP = 0.1
PAD = 8
OP = 16
LANES = 128
REACH = 12

FIRST = [(x, y, z) for x in (-1, 0) for y in (-1, 0) for z in (-1, 0)]
SECOND = [(1, 0, 0), (-1, 0, 0), (0, 1, 0), (0, -1, 0), (0, 0, 1), (0, 0, -1)]


def bonds(a):
    sign = 1 if a == 0 else -1
    first = [(1 - a, sign * x, sign * y, sign * z) for x, y, z in FIRST]
    return first + [(a, *e) for e in SECOND]


def mate_of(o):
    return o if o < 8 else 8 + ((o - 8) ^ 1)


def versions(a):
    s = 1 if a == 0 else -1
    return [(0, 0), (s, 0), (0, s), (s, s), (-s, 0), (0, -s)]


class Plane:
    def __init__(self, gx, yz, bx, by, rows=8):
        self.bx, self.by, self.yz, self.cells = bx, by, yz, bx * by
        self.nl = gx * yz * bx * by
        self.nt = self.nl // LANES
        self.lane = lax.broadcasted_iota(jnp.int32, (rows, LANES), 1)
        self.rows = rows

    def at(self, t):
        lane = self.lane + t * LANES
        return (lane // self.by) % self.bx, lane % self.by, (lane // self.cells) % self.yz

    def roll(self, v, s):
        s = s % self.nl
        q, r = divmod(s, LANES)
        nt = self.nt
        if r == 0:
            return [v[(t + q) % nt] for t in range(nt)]
        rot = [pltpu.roll(x, LANES - r, axis=1) for x in v]
        if nt == 1:
            return rot
        keep = self.lane < LANES - r
        return [jnp.where(keep, rot[(t + q) % nt], rot[(t + q + 1) % nt]) for t in range(nt)]

    def step_x(self, v, d):
        if d == 0:
            return v
        ring = self.cells * self.yz
        inner = self.roll(v, d * self.by)
        outer = self.roll(v, d * (ring - (self.bx - 1) * self.by))
        edge = self.bx - 1 if d > 0 else 0
        return [jnp.where(self.at(t)[0] == edge, outer[t], inner[t]) for t in range(self.nt)]

    def step_y(self, v, d):
        if d == 0:
            return v
        ring = self.cells * self.yz
        hop = d * (self.cells - (self.by - 1))
        inner = self.roll(v, d)
        outer = self.roll(v, hop)
        wrap = self.roll(v, hop - d * ring)
        edge = self.by - 1 if d > 0 else 0
        last = self.yz - 1 if d > 0 else 0
        out = []
        for t in range(self.nt):
            _, yl, brick = self.at(t)
            far = jnp.where(brick == last, wrap[t], outer[t])
            out.append(jnp.where(yl == edge, far, inner[t]))
        return out

    def step(self, v, dx, dy):
        return self.step_x(self.step_y(v, dy), dx)


def split(x):
    hi = x.astype(jnp.bfloat16)
    return hi, (x - hi.astype(jnp.float32)).astype(jnp.bfloat16)


def pack_kernel(n, sz, rep, half, halo, x_ref, out_ref, ext):
    rows, cz = x_ref.shape
    x = jnp.concatenate([x_ref[...], jnp.zeros((LANES - rows, cz), jnp.float32)], 0)
    cells = x.T
    ext[pl.ds(0, cz), :] = cells
    ext[pl.ds(cz, half), :] = cells[:half]
    upper = pltpu.roll(ext[pl.ds(half, cz), :], LANES // 2, axis=1)
    lane = lax.broadcasted_iota(jnp.int32, (cz, LANES), 1)
    both = jnp.where(lane < LANES // 2, cells, upper)
    ext[pl.ds(half, cz), :] = both
    ext[pl.ds(0, half), :] = both[cz - half :]

    def send(d, carry):
        start = (d // rep) * sz - halo + half
        out_ref[d] = ext[pl.ds(start, half), :]
        return carry

    lax.fori_loop(0, n, send, 0, unroll=8)


def unpack_kernel(in_ref, out_ref):
    out_ref[...] = in_ref[...].T[: out_ref.shape[0]]


def sweep_kernel(
    gx, yz, bx, by, cz, sz, rep, half, halo,
    recv_ref, pair_ref, mix_ref, bias_ref, outw_ref,
    out_ref,
    spin, spin2, ver, cosv, grad, w1, w2, bias,
):
    pp = Plane(gx, yz, bx, by)
    nt, cells = pp.nt, pp.cells
    rows = spin.shape[2]
    stride = 2 * rows
    blk = LANES // cells
    window = 2 * half

    parts = []
    for k in range(NB):
        part = pair_ref[pl.ds(k, 14, stride=NB), :]
        parts.append(jnp.concatenate([part, jnp.zeros((OP - 14, part.shape[1]), jnp.float32)], 0))
    pair = jnp.concatenate(parts, 0)
    w = jnp.dot(pair, mix_ref[...], precision=lax.Precision.HIGHEST, preferred_element_type=jnp.float32)
    hi, lo = split(w.T)
    w1[...] = jnp.concatenate(
        [jnp.concatenate([hi, hi], 1), jnp.concatenate([lo, lo], 1)], 0
    )
    degree = lax.broadcasted_iota(jnp.int32, w.shape, 0) // OP + 1
    hi, lo = split(w * degree.astype(jnp.float32) * outw_ref[...])
    w2[...] = jnp.concatenate(
        [jnp.concatenate([hi, hi], 1), jnp.concatenate([lo, lo], 1)], 0
    )
    bias[...] = jnp.broadcast_to(bias_ref[...], (LANES, bias_ref.shape[1])).T

    lane16 = lax.broadcasted_iota(jnp.int32, (half, LANES), 1) // cells

    def gather(t, carry):
        moved = []
        for k in range(blk):
            v = recv_ref[t * blk + k]
            moved.append(pltpu.roll(v, k * cells, axis=1) if k else v)
        for ca in range(6):
            for h in range(2):
                j = ca + h * (LANES // 2 // cells)
                u = moved[0]
                for k in range(1, blk):
                    u = jnp.where(lane16 == (j + k) % blk, moved[k], u)
                if j:
                    u = pltpu.roll(u, LANES - j * cells, axis=1)
                spin[ca, t, pl.ds(PAD + h * half, half), :] = u
                spin2[ca, t, pl.ds(PAD + h * half, half), :] = u
        return carry

    if nt <= 2:
        for t in range(nt):
            gather(t, 0)
    else:
        lax.fori_loop(0, nt, gather, 0)
    for t in range(nt):
        cosv[t, pl.ds(14 * stride, 2 * stride), :] = jnp.zeros((2 * stride, LANES), jnp.float32)

    me = lax.axis_index("gx") * yz + lax.axis_index("yz")
    z0 = (me // rep) * sz
    hz = cz // 2
    zs = (z0 - halo + cz) % cz
    first = ((zs + hz - 1) // hz) * hz
    inside = first - zs < window
    border = PAD + first - zs
    hi_above = first % cz == hz
    own = PAD + halo

    def is_hi(row):
        z = row - PAD + zs
        z = jnp.where(z >= cz, z - cz, z)
        return z >= hz

    low, high = own - 2, own + sz + 2
    ranges = []
    for _ in range(4):
        near_low = inside & hi_above & (border > low - 2) & (border < low + 2)
        near_high = inside & jnp.logical_not(hi_above) & (border > high - 2) & (border < high + 2)
        f_low = jnp.where(near_low, low - 2, low)
        f_high = jnp.where(near_high, high + 2, high)
        ranges.append((f_low, f_high))
        low, high = f_low - 2, f_high + 2
    ranges = ranges[::-1]

    def shifted_spins(start, count):
        def body(i, carry):
            r = start + 8 * i
            for ca in range(6):
                v = [spin[ca, t, pl.ds(r, 8), :] for t in range(nt)]
                a = ca % 2
                xs = {}
                for n, (dx, dy) in enumerate(versions(a)):
                    if n == 0:
                        continue
                    if dx and dy:
                        got = pp.step_x(xs[(0, dy)], dx)
                    else:
                        got = pp.step(v, dx, dy)
                    xs[(dx, dy)] = got
                    for t in range(nt):
                        ver[n - 1, ca, t, pl.ds(r, 8), :] = got[t]
            return carry

        lax.fori_loop(0, count, body, 0)

    def neighbour(c, a, dx, dy, t, r):
        n = versions(a).index((dx, dy))
        if n == 0:
            return spin[2 * c + a, t, pl.ds(r, 8), :]
        return ver[n - 1, 2 * c + a, t, pl.ds(r, 8), :]

    def cosines(start, count):
        def body(i, carry):
            r = start + 8 * i
            for t in range(nt):
                for a in range(2):
                    mine = [spin[2 * c + a, t, pl.ds(r, 8), :] for c in range(3)]
                    for o, (b, dx, dy, dz) in enumerate(bonds(a)):
                        total = mine[0] * neighbour(0, b, dx, dy, t, r + dz)
                        for c in (1, 2):
                            total += mine[c] * neighbour(c, b, dx, dy, t, r + dz)
                        cosv[t, pl.ds(o * stride + a * rows + r, 8), :] = total
            return carry

        lax.fori_loop(0, count, body, 0)

    tc = 2 if nt % 2 == 0 else 1
    chunks = nt // tc

    def gradients(start, count):
        def body(i, carry):
            if chunks == 1:
                r, t0 = start + 2 * i, 0
            else:
                r, t0 = start + 2 * (i // chunks), (i % chunks) * tc
            places = [(d, a, t) for d in range(2) for a in range(2) for t in range(tc)]
            c = jnp.concatenate(
                [cosv[t0 + t, pl.ds(a * rows + r + d, OP, stride=stride), :] for d, a, t in places], 1
            )
            c2 = c + c
            kinds = [c, c2 * c - 1.0]
            for _ in range(2, NB):
                kinds.append(c2 * kinds[-1] - kinds[-2])
            f_hi, f_lo = split(jnp.concatenate(kinds, 0))
            z = jnp.dot(w1[...], jnp.concatenate([f_hi, f_lo], 0), preferred_element_type=jnp.float32)
            hid = z[:LANES] + z[LANES:]
            hid = hid + jnp.concatenate([bias[...]] * len(places), 1)
            u = jnp.tanh(hid)
            d_hi, d_lo = split(1.0 - u * u)
            y = jnp.dot(w2[...], jnp.concatenate([d_hi, d_lo], 0), preferred_element_type=jnp.float32)
            y = y[:LANES] + y[LANES:]
            b1 = y[(NB - 1) * OP :]
            b2 = None
            for k in range(NB - 2, -1, -1):
                new = y[k * OP : (k + 1) * OP] + c2 * b1
                if b2 is not None:
                    new = new - b2
                b1, b2 = new, b1
            for n, (d, a, t) in enumerate(places):
                grad[t0 + t, pl.ds(a * rows + r + d, OP, stride=stride), :] = b1[:, n * LANES : (n + 1) * LANES]
            return carry

        lax.fori_loop(0, count * chunks, body, 0)

    def field(r):
        out = []
        for a in range(2):
            total = [[None] * nt for _ in range(3)]
            for o, (b, dx, dy, dz) in enumerate(bonds(a)):
                m = mate_of(o)
                theirs = [grad[t, pl.ds(m * stride + b * rows + r + dz, 8), :] for t in range(nt)]
                theirs = pp.step(theirs, dx, dy)
                for t in range(nt):
                    coeff = grad[t, pl.ds(o * stride + a * rows + r, 8), :] + theirs[t]
                    for c in range(3):
                        term = coeff * neighbour(c, b, dx, dy, t, r + dz)
                        total[c][t] = term if total[c][t] is None else total[c][t] + term
            out.append([[-x for x in per] for per in total])
        return out

    def update(start, count, stage, only_border):
        def body(i, carry):
            r = start + 8 * i
            row = lax.broadcasted_iota(jnp.int32, (8, LANES), 0) + r
            from_border = jnp.where(hi_above, row - border, border - 1 - row)
            wanted = jnp.logical_not(only_border) | ((from_border >= 0) & (from_border < 2))
            h = field(r)
            for a in range(2):
                for t in range(nt):
                    xl, yl, _ = pp.at(t)
                    mask = (
                        ((xl >= bx // 2).astype(jnp.int32) == stage // 2)
                        & ((yl >= by // 2).astype(jnp.int32) == stage % 2)
                        & wanted
                    )
                    s = [spin[2 * c + a, t, pl.ds(r, 8), :] for c in range(3)]
                    w = [TIME_STEP * h[a][c][t] for c in range(3)]
                    half_r = 0.5 * jnp.sqrt(w[0] * w[0] + w[1] * w[1] + w[2] * w[2])
                    sn, cs = jnp.sin(half_r), jnp.cos(half_r)
                    zero = half_r == 0.0
                    hs = jnp.where(zero, 1.0, sn / jnp.where(zero, 1.0, half_r))
                    cosr = 1.0 - 2.0 * sn * sn
                    sinc = hs * cs
                    proj = 0.5 * hs * hs * (w[0] * s[0] + w[1] * s[1] + w[2] * s[2])
                    for c in range(3):
                        p, q = (c + 1) % 3, (c + 2) % 3
                        cross = w[p] * s[q] - w[q] * s[p]
                        new = cosr * s[c] + sinc * cross + proj * w[c]
                        old = spin2[2 * c + a, t, pl.ds(r, 8), :]
                        spin2[2 * c + a, t, pl.ds(r, 8), :] = jnp.where(mask, new, old)
            return carry

        lax.fori_loop(0, count, body, 0)

    def take(everything):
        for i in range(window // 8):
            r = PAD + 8 * i
            row = lax.broadcasted_iota(jnp.int32, (8, LANES), 0) + r
            sel = everything | jnp.logical_not(is_hi(row))
            for ca in range(6):
                for t in range(nt):
                    place = (ca, t, pl.ds(r, 8), slice(None))
                    spin[place] = jnp.where(sel, spin2[place], spin[place])

    def phase(p, carry):
        stage, fix = p // 2, p % 2 == 1
        f_low, f_high = ranges[0]
        for s in range(1, 5):
            lo_s, hi_s = ranges[s] if s < 4 else (own, own + sz)
            f_low = jnp.where(stage == s, lo_s, f_low)
            f_high = jnp.where(stage == s, hi_s, f_high)
        n = f_high - f_low
        last = stage == 4
        crosses = inside & (f_low < border) & (border < f_high)

        @pl.when(jnp.logical_not(fix) | crosses)
        def _():
            shifted_spins(jnp.where(fix, border - 4, f_low - 2), jnp.where(fix, 1, (n + 11) // 8))
            cosines(jnp.where(fix, border - 4, f_low - 1), jnp.where(fix, 1, (n + 9) // 8))
            gradients(jnp.where(fix, border - 1, f_low - 1), jnp.where(fix, 1, (n + 3) // 2))

            @pl.when(jnp.logical_not(last))
            def _():
                update(
                    jnp.where(fix, border - 4, f_low), jnp.where(fix, 1, (n + 7) // 8), stage, fix
                )
                take(fix | jnp.logical_not(crosses))

        return carry

    lax.fori_loop(0, 9, phase, 0)

    final = field(own)
    lane16s = lax.broadcasted_iota(jnp.int32, (8, LANES), 1) // cells
    for t in range(nt):
        moved = []
        for j in range(12):
            ca = j % 6
            v = spin[ca, t, pl.ds(own, 8), :] if j < 6 else final[ca % 2][ca // 2][t]
            moved.append(pltpu.roll(v, j * cells, axis=1) if j else v)
        for k in range(blk):
            u = moved[0]
            for j in range(1, 12):
                u = jnp.where(lane16s == (j + k) % blk, moved[j], u)
            if k:
                u = pltpu.roll(u, LANES - k * cells, axis=1)
            out_ref[t * blk + k] = u[:sz]


def per_device(gx, yz, spin_vectors, pair_weight, mix_weight, mix_bias, out_weight):
    three, two, bx, by, cz = spin_vectors.shape
    n = gx * yz
    sz = max(1, cz // n)
    rep = n * sz // cz
    half = -(-(sz + 2 * REACH) // 16) * 8
    halo = (2 * half - sz) // 2
    rows = 2 * half + 2 * PAD
    nt = n * bx * by // LANES
    brick = three * two * bx * by
    vmem = pl.BlockSpec(memory_space=pltpu.VMEM)

    packed = pl.pallas_call(
        functools.partial(pack_kernel, n, sz, rep, half, halo),
        out_shape=jax.ShapeDtypeStruct((n, half, LANES), jnp.float32),
        in_specs=[vmem],
        out_specs=vmem,
        scratch_shapes=[pltpu.VMEM((cz + 2 * half, LANES), jnp.float32)],
        name="pack",
    )(spin_vectors.reshape(brick, cz))
    received = lax.all_to_all(packed, ("gx", "yz"), 0, 0, tiled=True)

    f32, bf16 = jnp.float32, jnp.bfloat16
    result = pl.pallas_call(
        functools.partial(sweep_kernel, gx, yz, bx, by, cz, sz, rep, half, halo),
        out_shape=jax.ShapeDtypeStruct((n, sz, LANES), f32),
        in_specs=[vmem] * 5,
        out_specs=vmem,
        scratch_shapes=[
            pltpu.VMEM((6, nt, rows, LANES), f32),
            pltpu.VMEM((6, nt, rows, LANES), f32),
            pltpu.VMEM((5, 6, nt, rows, LANES), f32),
            pltpu.VMEM((nt, OP * 2 * rows, LANES), f32),
            pltpu.VMEM((nt, OP * 2 * rows, LANES), f32),
            pltpu.VMEM((2 * LANES, 2 * LANES), bf16),
            pltpu.VMEM((2 * LANES, 2 * LANES), bf16),
            pltpu.VMEM((LANES, LANES), f32),
        ],
        compiler_params=pltpu.CompilerParams(vmem_limit_bytes=58 * 2**20),
        name="sweep",
    )(received, pair_weight, mix_weight, mix_bias[None], out_weight[None])
    returned = lax.all_to_all(result, ("gx", "yz"), 0, 0, tiled=True)
    if rep > 1:
        returned = returned[::rep]

    both = pl.pallas_call(
        unpack_kernel,
        out_shape=jax.ShapeDtypeStruct((2 * brick, cz), f32),
        in_specs=[vmem],
        out_specs=vmem,
        name="unpack",
    )(returned.reshape(cz, LANES))
    both = both.reshape(2, three, two, bx, by, cz)
    return both[0], both[1]


def solution(mesh):
    gx, yz = mesh.shape["gx"], mesh.shape["yz"]
    spec = P(None, None, "gx", "yz", None)
    return jax.shard_map(
        functools.partial(per_device, gx, yz),
        mesh=mesh,
        in_specs=(spec, P(), P(), P(), P()),
        out_specs=(spec, spec),
        check_vma=False,
    )
```

profile of v0, /device:TPU:0, one launch (start us, length us, event | category | flops | bytes accessed | tf_op | source)
XLA Modules:
  0.0 72.4 jit_solution(14074511808105963868)
XLA Ops:
  0.6 1.6 %pack.1 = f32[32,16,128]{2,1,0:T(8,128)} custom-call(f32[48,128]{1,0:T(8,128)} %bitcast.7), custom_call_target="tpu_custom_call" | custom-call | tf_op jit(solution)/shard_map/pack/pallas_call | solution.py:399
  2.3 17.8 %all_to_all.10.recv_ref = f32[32,16,128]{2,1,0:T(8,128)} all-to-all(f32[32,16,128]{2,1,0:T(8,128)} %pack.1), channel_id=1, replica_groups=mesh['gx'=4,'yz'=8] {'gx','yz'}, dimensions={0} | all-to-all | bytes 524288 | tf_op jit(solution)/shard_map/all_to_all | solution.py:407
  20.1 38.0 %sweep.1 = f32[32,4,128]{2,1,0:T(4,128)} custom-call(f32[32,16,128]{2,1,0:T(8,128)} %all_to_all.10.recv_ref, f32[112,128]{1,0:T(8,128)} %pair_ref.1, f32[128,128]{1,0:T(8,128)} %mix_ref.1, f32[1,128]{1,0:T(1,128)} %bitcast.10, f32[1,128]{1,0:T(1,128)} %bitcast.11), custom_call_target="tpu_custom_call" | custom-call | tf_op jit(solution)/shard_map/sweep/pallas_call | solution.py:410
  58.0 11.5 %all_to_all.11 = f32[32,4,128]{2,1,0:T(4,128)} all-to-all(f32[32,4,128]{2,1,0:T(4,128)} %sweep.1), channel_id=1, replica_groups=mesh['gx'=4,'yz'=8] {'gx','yz'}, dimensions={0} | all-to-all | bytes 131072 | tf_op jit(solution)/shard_map/all_to_all | solution.py:428
  69.5 1.5 %unpack.1 = f32[96,128]{1,0:T(8,128)} custom-call(f32[128,128]{1,0:T(8,128)} %bitcast.6), custom_call_target="tpu_custom_call" | custom-call | tf_op jit(solution)/shard_map/unpack/pallas_call | solution.py:432
  71.1 1.4 %fusion = (f32[48,128]{1,0:T(8,128)}, f32[48,128]{1,0:T(8,128)}) fusion(f32[96,128]{1,0:T(8,128)} %unpack.1), kind=kLoop, calls=%fused_computation | loop fusion | bytes 98304 | tf_op jit(solution)/shard_map/slice | solution.py:440
where the time goes:
time: 72.9 us; the launch traced here: 72.4 us
  Pallas kernels  41.1 us (56%)
  blocking collectives  29.3 us (40%)
  local copies, waits for them, and re-layouts  1.37 us (2%)
    pallas_call x1, Pallas kernels, per_device(): pl.pallas_call(functools.partial(sweep_kernel, gx, yz, bx, by, cz, sz, re...  38 us
    all_to_all x1, blocking collectives, per_device(): received = lax.all_to_all(packed, ('gx', 'yz'), 0, 0, tiled=True)  17.8 us
    all_to_all x1, blocking collectives, per_device(): returned = lax.all_to_all(result, ('gx', 'yz'), 0, 0, tiled=True)  11.5 us
    pallas_call x1, Pallas kernels, per_device(): pl.pallas_call(functools.partial(pack_kernel, n, sz, rep, half, halo), ou...  1.63 us
    pallas_call x1, Pallas kernels, per_device(): pl.pallas_call(unpack_kernel, out_shape=jax.ShapeDtypeStruct((2 * brick,...  1.54 us

commit v1 on v0

--- a/solution.py
+++ b/solution.py
@@ -1,4 +1,5 @@
 import functools
+import math
 
 import jax
 import jax.numpy as jnp
@@ -92,6 +93,21 @@
     return hi, (x - hi.astype(jnp.float32)).astype(jnp.bfloat16)
 
 
+def half_turn(square):
+    v = jnp.sqrt(square)
+    n = jnp.round(v * (1.0 / math.pi))
+    p = ((v - n * 3.140625) - n * 9.67502593994140625e-4) - n * 1.5099579909783764e-7
+    s = p * p
+    sine, cosine = -1.0 / 39916800, 1.0 / 479001600
+    for k in (9, 7, 5, 3, 1):
+        sine = sine * s + (-1.0) ** (k // 2) / math.factorial(k)
+    for k in (10, 8, 6, 4, 2, 0):
+        cosine = cosine * s + (-1.0) ** (k // 2) / math.factorial(k)
+    sn = sine * p
+    small = n == 0.0
+    return sn, cosine, jnp.where(small, sine, sn / jnp.where(small, 1.0, v))
+
+
 def pack_kernel(n, sz, rep, half, halo, x_ref, out_ref, ext):
     rows, cz = x_ref.shape
     x = jnp.concatenate([x_ref[...], jnp.zeros((LANES - rows, cz), jnp.float32)], 0)
@@ -112,20 +128,23 @@
     lax.fori_loop(0, n, send, 0, unroll=8)
 
 
-def unpack_kernel(in_ref, out_ref):
-    out_ref[...] = in_ref[...].T[: out_ref.shape[0]]
+def unpack_kernel(in_ref, spin_ref, field_ref):
+    x = in_ref[...].T
+    n = spin_ref.shape[0]
+    spin_ref[...] = x[:n]
+    field_ref[...] = x[n : 2 * n]
 
 
 def sweep_kernel(
     gx, yz, bx, by, cz, sz, rep, half, halo,
     recv_ref, pair_ref, mix_ref, bias_ref, outw_ref,
     out_ref,
-    spin, spin2, ver, cosv, grad, w1, w2, bias,
+    spin, spin2, ver, cosv, grad, w1, w2, hidden,
 ):
     pp = Plane(gx, yz, bx, by)
     nt, cells = pp.nt, pp.cells
     rows = spin.shape[2]
-    stride = 2 * rows
+    stride = 2 * rows + 1
     blk = LANES // cells
     window = 2 * half
 
@@ -135,7 +154,11 @@
         parts.append(jnp.concatenate([part, jnp.zeros((OP - 14, part.shape[1]), jnp.float32)], 0))
     pair = jnp.concatenate(parts, 0)
     w = jnp.dot(pair, mix_ref[...], precision=lax.Precision.HIGHEST, preferred_element_type=jnp.float32)
-    hi, lo = split(w.T)
+    row = lax.broadcasted_iota(jnp.int32, w.shape, 0)
+    shift = bias_ref[...]
+    rest = shift - split(shift)[0].astype(jnp.float32)
+    rest = rest - split(rest)[0].astype(jnp.float32)
+    hi, lo = split(jnp.where(row == 14, shift, jnp.where(row == 15, rest, w)).T)
     w1[...] = jnp.concatenate(
         [jnp.concatenate([hi, hi], 1), jnp.concatenate([lo, lo], 1)], 0
     )
@@ -144,7 +167,6 @@
     w2[...] = jnp.concatenate(
         [jnp.concatenate([hi, hi], 1), jnp.concatenate([lo, lo], 1)], 0
     )
-    bias[...] = jnp.broadcast_to(bias_ref[...], (LANES, bias_ref.shape[1])).T
 
     lane16 = lax.broadcasted_iota(jnp.int32, (half, LANES), 1) // cells
 
@@ -171,7 +193,7 @@
     else:
         lax.fori_loop(0, nt, gather, 0)
     for t in range(nt):
-        cosv[t, pl.ds(14 * stride, 2 * stride), :] = jnp.zeros((2 * stride, LANES), jnp.float32)
+        cosv[t, pl.ds(14 * stride, 2 * stride), :] = jnp.ones((2 * stride, LANES), jnp.float32)
 
     me = lax.axis_index("gx") * yz + lax.axis_index("yz")
     z0 = (me // rep) * sz
@@ -245,27 +267,44 @@
     chunks = nt // tc
 
     def gradients(start, count):
-        def body(i, carry):
+        places = [(d, a, t) for d in range(2) for a in range(2) for t in range(tc)]
+
+        def place(i):
             if chunks == 1:
-                r, t0 = start + 2 * i, 0
-            else:
-                r, t0 = start + 2 * (i // chunks), (i % chunks) * tc
-            places = [(d, a, t) for d in range(2) for a in range(2) for t in range(tc)]
-            c = jnp.concatenate(
+                return start + 2 * i, 0
+            return start + 2 * (i // chunks), (i % chunks) * tc
+
+        def cosine(i):
+            r, t0 = place(i)
+            return jnp.concatenate(
                 [cosv[t0 + t, pl.ds(a * rows + r + d, OP, stride=stride), :] for d, a, t in places], 1
             )
+
+        def basis(i):
+            c = cosine(i)
             c2 = c + c
             kinds = [c, c2 * c - 1.0]
             for _ in range(2, NB):
                 kinds.append(c2 * kinds[-1] - kinds[-2])
             f_hi, f_lo = split(jnp.concatenate(kinds, 0))
-            z = jnp.dot(w1[...], jnp.concatenate([f_hi, f_lo], 0), preferred_element_type=jnp.float32)
-            hid = z[:LANES] + z[LANES:]
-            hid = hid + jnp.concatenate([bias[...]] * len(places), 1)
-            u = jnp.tanh(hid)
+            return jnp.concatenate([f_hi, f_lo], 0)
+
+        def forward(rhs):
+            z = jnp.dot(w1[...], rhs, preferred_element_type=jnp.float32)
+            hidden[...] = z[:LANES] + z[LANES:]
+
+        def activate():
+            u = jnp.tanh(hidden[...])
             d_hi, d_lo = split(1.0 - u * u)
-            y = jnp.dot(w2[...], jnp.concatenate([d_hi, d_lo], 0), preferred_element_type=jnp.float32)
-            y = y[:LANES] + y[LANES:]
+            return jnp.concatenate([d_hi, d_lo], 0)
+
+        def backward(rhs):
+            y = jnp.dot(w2[...], rhs, preferred_element_type=jnp.float32)
+            return y[:LANES] + y[LANES:]
+
+        def combine(i, y):
+            r, t0 = place(i)
+            c2 = 2.0 * cosine(i)
             b1 = y[(NB - 1) * OP :]
             b2 = None
             for k in range(NB - 2, -1, -1):
@@ -275,9 +314,19 @@
                 b1, b2 = new, b1
             for n, (d, a, t) in enumerate(places):
                 grad[t0 + t, pl.ds(a * rows + r + d, OP, stride=stride), :] = b1[:, n * LANES : (n + 1) * LANES]
+
+        forward(basis(0))
+
+        def body(i, carry):
+            rhs2 = activate()
+            rhs1 = basis(i)
+            y = backward(rhs2)
+            forward(rhs1)
+            combine(i - 1, y)
             return carry
 
-        lax.fori_loop(0, count * chunks, body, 0)
+        lax.fori_loop(1, count * chunks, body, 0)
+        combine(count * chunks - 1, backward(activate()))
 
     def field(r):
         out = []
@@ -312,10 +361,8 @@
                     )
                     s = [spin[2 * c + a, t, pl.ds(r, 8), :] for c in range(3)]
                     w = [TIME_STEP * h[a][c][t] for c in range(3)]
-                    half_r = 0.5 * jnp.sqrt(w[0] * w[0] + w[1] * w[1] + w[2] * w[2])
-                    sn, cs = jnp.sin(half_r), jnp.cos(half_r)
-                    zero = half_r == 0.0
-                    hs = jnp.where(zero, 1.0, sn / jnp.where(zero, 1.0, half_r))
+                    square = 0.25 * (w[0] * w[0] + w[1] * w[1] + w[2] * w[2])
+                    sn, cs, hs = half_turn(square)
                     cosr = 1.0 - 2.0 * sn * sn
                     sinc = hs * cs
                     proj = 0.5 * hs * hs * (w[0] * s[0] + w[1] * s[1] + w[2] * s[2])
@@ -416,11 +463,11 @@
             pltpu.VMEM((6, nt, rows, LANES), f32),
             pltpu.VMEM((6, nt, rows, LANES), f32),
             pltpu.VMEM((5, 6, nt, rows, LANES), f32),
-            pltpu.VMEM((nt, OP * 2 * rows, LANES), f32),
-            pltpu.VMEM((nt, OP * 2 * rows, LANES), f32),
+            pltpu.VMEM((nt, OP * (2 * rows + 1) + 7, LANES), f32),
+            pltpu.VMEM((nt, OP * (2 * rows + 1) + 7, LANES), f32),
             pltpu.VMEM((2 * LANES, 2 * LANES), bf16),
             pltpu.VMEM((2 * LANES, 2 * LANES), bf16),
-            pltpu.VMEM((LANES, LANES), f32),
+            pltpu.VMEM((LANES, 4 * (2 - nt % 2) * LANES), f32),
         ],
         compiler_params=pltpu.CompilerParams(vmem_limit_bytes=58 * 2**20),
         name="sweep",
@@ -429,15 +476,14 @@
     if rep > 1:
         returned = returned[::rep]
 
-    both = pl.pallas_call(
+    outs = pl.pallas_call(
         unpack_kernel,
-        out_shape=jax.ShapeDtypeStruct((2 * brick, cz), f32),
+        out_shape=[jax.ShapeDtypeStruct((brick, cz), f32)] * 2,
         in_specs=[vmem],
-        out_specs=vmem,
+        out_specs=[vmem] * 2,
         name="unpack",
     )(returned.reshape(cz, LANES))
-    both = both.reshape(2, three, two, bx, by, cz)
-    return both[0], both[1]
+    return tuple(x.reshape(three, two, bx, by, cz) for x in outs)
 
 
 def solution(mesh):

time: 72.9 us -> 66.6 us (0.914)
  Pallas kernels: 41.1 us -> 36.8 us
  local copies, waits for them, and re-layouts: 1.37 us -> 0 us
    pallas_call x1, Pallas kernels: 38 us -> 33.6 us  [per_device(): pl.pallas_call(functools.partial(sweep_kernel, gx, yz, bx, by, cz, sz, re...]
    slice x1 -> x0, local copies, waits for them, and re-layouts: 1.37 us -> none  [per_device(): return (both[0], both[1])]
where the time goes in v1:
time: 66.6 us; the launch traced here: 66.2 us
  Pallas kernels  36.8 us (55%)
  blocking collectives  28.8 us (43%)
    pallas_call x1, Pallas kernels, per_device(): pl.pallas_call(functools.partial(sweep_kernel, gx, yz, bx, by, cz, sz, re...  33.6 us
    all_to_all x1, blocking collectives, per_device(): received = lax.all_to_all(packed, ('gx', 'yz'), 0, 0, tiled=True)  17.8 us
    all_to_all x1, blocking collectives, per_device(): returned = lax.all_to_all(result, ('gx', 'yz'), 0, 0, tiled=True)  11 us
    pallas_call x1, Pallas kernels, per_device(): pl.pallas_call(functools.partial(pack_kernel, n, sz, rep, half, halo), ou...  1.63 us
    pallas_call x1, Pallas kernels, per_device(): pl.pallas_call(unpack_kernel, out_shape=[jax.ShapeDtypeStruct((brick, cz)...  1.54 us

profile of v1, /device:TPU:0, one launch (start us, length us, event | category | flops | bytes accessed | tf_op | source)
XLA Modules:
  0.0 66.2 jit_solution(10485756340841484943)
XLA Ops:
  0.6 1.6 %pack.1 = f32[32,16,128]{2,1,0:T(8,128)} custom-call(f32[48,128]{1,0:T(8,128)} %bitcast.7), custom_call_target="tpu_custom_call" | custom-call | tf_op jit(solution)/shard_map/pack/pallas_call | solution.py:446
  2.3 17.8 %all_to_all.10.recv_ref = f32[32,16,128]{2,1,0:T(8,128)} all-to-all(f32[32,16,128]{2,1,0:T(8,128)} %pack.1), channel_id=1, replica_groups=mesh['gx'=4,'yz'=8] {'gx','yz'}, dimensions={0} | all-to-all | bytes 524288 | tf_op jit(solution)/shard_map/all_to_all | solution.py:454
  20.1 33.6 %sweep.1 = f32[32,4,128]{2,1,0:T(4,128)} custom-call(f32[32,16,128]{2,1,0:T(8,128)} %all_to_all.10.recv_ref, f32[112,128]{1,0:T(8,128)} %pair_ref.1, f32[128,128]{1,0:T(8,128)} %mix_ref.1, f32[1,128]{1,0:T(1,128)} %bitcast.8, f32[1,128]{1,0:T(1,128)} %bitcast.9), custom_call_target="tpu_custom_call" | custom-call | tf_op jit(solution)/shard_map/sweep/pallas_call | solution.py:457
  53.7 11.0 %all_to_all.11 = f32[32,4,128]{2,1,0:T(4,128)} all-to-all(f32[32,4,128]{2,1,0:T(4,128)} %sweep.1), channel_id=1, replica_groups=mesh['gx'=4,'yz'=8] {'gx','yz'}, dimensions={0} | all-to-all | bytes 131072 | tf_op jit(solution)/shard_map/all_to_all | solution.py:475
  64.7 1.5 %unpack.1 = (f32[48,128]{1,0:T(8,128)}, f32[48,128]{1,0:T(8,128)}) custom-call(f32[128,128]{1,0:T(8,128)} %bitcast.6), custom_call_target="tpu_custom_call" | custom-call | tf_op jit(solution)/shard_map/unpack/pallas_call | solution.py:479

commit v2 on v1

--- a/solution.py
+++ b/solution.py
@@ -40,7 +40,19 @@
         self.nl = gx * yz * bx * by
         self.nt = self.nl // LANES
         self.lane = lax.broadcasted_iota(jnp.int32, (rows, LANES), 1)
-        self.rows = rows
+        ring = yz * self.cells
+        self.within = LANES % ring == 0
+        if self.within:
+            xl, yl, brick = self.at(0)
+            x_at = {0: self.lane, 1: jnp.where(xl == bx - 1, self.lane + ring - (bx - 1) * by, self.lane + by),
+                    -1: jnp.where(xl == 0, self.lane - ring + (bx - 1) * by, self.lane - by)}
+            hop = self.cells - (by - 1)
+            y_at = {0: 0, 1: jnp.where(yl < by - 1, 1, jnp.where(brick < yz - 1, hop, hop - ring)),
+                    -1: jnp.where(yl > 0, -1, jnp.where(brick > 0, -hop, ring - hop))}
+            self.source = {
+                (dx, dy): (x_at[dx] + y_at[dy] + LANES) % LANES for dx in (-1, 0, 1) for dy in (-1, 0, 1)
+            }
+            self.from_next = {1: (self.lane < ring) & (xl == 0), -1: (self.lane >= LANES - ring) & (xl == bx - 1)}
 
     def at(self, t):
         lane = self.lane + t * LANES
@@ -85,6 +97,14 @@
         return out
 
     def step(self, v, dx, dy):
+        if not (dx or dy):
+            return v
+        if self.within:
+            if dx and self.nt > 1:
+                swap = self.from_next[dx]
+                v = [jnp.where(swap, v[(t + dx) % self.nt], v[t]) for t in range(self.nt)]
+            where = self.source[(dx, dy)]
+            return [jnp.take_along_axis(x, where, axis=1, mode="promise_in_bounds") for x in v]
         return self.step_x(self.step_y(v, dy), dx)
 
 
@@ -224,18 +244,12 @@
     def shifted_spins(start, count):
         def body(i, carry):
             r = start + 8 * i
-            for ca in range(6):
-                v = [spin[ca, t, pl.ds(r, 8), :] for t in range(nt)]
-                a = ca % 2
-                xs = {}
-                for n, (dx, dy) in enumerate(versions(a)):
-                    if n == 0:
+            for dx, dy in ((1, 0), (-1, 0), (0, 1), (0, -1), (1, 1), (-1, -1)):
+                for ca in range(6):
+                    if (dx, dy) not in versions(ca % 2):
                         continue
-                    if dx and dy:
-                        got = pp.step_x(xs[(0, dy)], dx)
-                    else:
-                        got = pp.step(v, dx, dy)
-                    xs[(dx, dy)] = got
+                    n = versions(ca % 2).index((dx, dy))
+                    got = pp.step([spin[ca, t, pl.ds(r, 8), :] for t in range(nt)], dx, dy)
                     for t in range(nt):
                         ver[n - 1, ca, t, pl.ds(r, 8), :] = got[t]
             return carry
@@ -267,12 +281,12 @@
     chunks = nt // tc
 
     def gradients(start, count):
-        places = [(d, a, t) for d in range(2) for a in range(2) for t in range(tc)]
+        places = [(d, a, t) for d in range(1) for a in range(2) for t in range(tc)]
 
         def place(i):
             if chunks == 1:
-                return start + 2 * i, 0
-            return start + 2 * (i // chunks), (i % chunks) * tc
+                return start + 1 * i, 0
+            return start + 1 * (i // chunks), (i % chunks) * tc
 
         def cosine(i):
             r, t0 = place(i)
@@ -289,12 +303,12 @@
             f_hi, f_lo = split(jnp.concatenate(kinds, 0))
             return jnp.concatenate([f_hi, f_lo], 0)
 
-        def forward(rhs):
+        def forward(rhs, slot):
             z = jnp.dot(w1[...], rhs, preferred_element_type=jnp.float32)
-            hidden[...] = z[:LANES] + z[LANES:]
-
-        def activate():
-            u = jnp.tanh(hidden[...])
+            hidden[slot] = z[:LANES] + z[LANES:]
+
+        def activate(slot):
+            u = jnp.tanh(hidden[slot])
             d_hi, d_lo = split(1.0 - u * u)
             return jnp.concatenate([d_hi, d_lo], 0)
 
@@ -315,18 +329,27 @@
             for n, (d, a, t) in enumerate(places):
                 grad[t0 + t, pl.ds(a * rows + r + d, OP, stride=stride), :] = b1[:, n * LANES : (n + 1) * LANES]
 
-        forward(basis(0))
-
-        def body(i, carry):
-            rhs2 = activate()
-            rhs1 = basis(i)
-            y = backward(rhs2)
-            forward(rhs1)
-            combine(i - 1, y)
-            return carry
-
-        lax.fori_loop(1, count * chunks, body, 0)
-        combine(count * chunks - 1, backward(activate()))
+        for k in range(2):
+            forward(basis(k), k)
+
+        def one(i, slot):
+            y = backward(activate(slot))
+            forward(basis(i), slot)
+            combine(i - 2, y)
+
+        total = count * chunks
+        done = 2
+        for many in (4, 2):
+            def body(i, first, many=many):
+                for k in range(many):
+                    one(first + i * many + k, k % 2)
+                return first
+
+            times = (total - done) // many
+            lax.fori_loop(0, times, body, done)
+            done = done + times * many
+        for k in range(2):
+            combine(total - 2 + k, backward(activate(k)))
 
     def field(r):
         out = []
@@ -401,7 +424,7 @@
         def _():
             shifted_spins(jnp.where(fix, border - 4, f_low - 2), jnp.where(fix, 1, (n + 11) // 8))
             cosines(jnp.where(fix, border - 4, f_low - 1), jnp.where(fix, 1, (n + 9) // 8))
-            gradients(jnp.where(fix, border - 1, f_low - 1), jnp.where(fix, 1, (n + 3) // 2))
+            gradients(jnp.where(fix, border - 1, f_low - 1), jnp.where(fix, 2, (n + 3) // 2 * 2))
 
             @pl.when(jnp.logical_not(last))
             def _():
@@ -467,7 +490,7 @@
             pltpu.VMEM((nt, OP * (2 * rows + 1) + 7, LANES), f32),
             pltpu.VMEM((2 * LANES, 2 * LANES), bf16),
             pltpu.VMEM((2 * LANES, 2 * LANES), bf16),
-            pltpu.VMEM((LANES, 4 * (2 - nt % 2) * LANES), f32),
+            pltpu.VMEM((2, LANES, 2 * (2 - nt % 2) * LANES), f32),
         ],
         compiler_params=pltpu.CompilerParams(vmem_limit_bytes=58 * 2**20),
         name="sweep",

time: 66.6 us -> 59.7 us (0.90)
  Pallas kernels: 36.8 us -> 30.1 us
    pallas_call x1, Pallas kernels: 33.6 us -> 26.9 us  [per_device(): pl.pallas_call(functools.partial(sweep_kernel, gx, yz, bx, by, cz, sz, re...]
where the time goes in v2:
time: 59.7 us; the launch traced here: 59.3 us
  Pallas kernels  30.1 us (50%)
  blocking collectives  28.6 us (48%)
  between operations  0.63 us (1%)
    pallas_call x1, Pallas kernels, per_device(): pl.pallas_call(functools.partial(sweep_kernel, gx, yz, bx, by, cz, sz, re...  26.9 us
    all_to_all x1, blocking collectives, per_device(): received = lax.all_to_all(packed, ('gx', 'yz'), 0, 0, tiled=True)  17.8 us
    all_to_all x1, blocking collectives, per_device(): returned = lax.all_to_all(result, ('gx', 'yz'), 0, 0, tiled=True)  10.8 us
    pallas_call x1, Pallas kernels, per_device(): pl.pallas_call(functools.partial(pack_kernel, n, sz, rep, half, halo), ou...  1.63 us
    pallas_call x1, Pallas kernels, per_device(): pl.pallas_call(unpack_kernel, out_shape=[jax.ShapeDtypeStruct((brick, cz)...  1.54 us

profile of v2, /device:TPU:0, one launch (start us, length us, event | category | flops | bytes accessed | tf_op | source)
XLA Modules:
  0.0 59.3 jit_solution(8222233456917643002)
XLA Ops:
  0.6 1.6 %pack.1 = f32[32,16,128]{2,1,0:T(8,128)} custom-call(f32[48,128]{1,0:T(8,128)} %bitcast.7), custom_call_target="tpu_custom_call" | custom-call | tf_op jit(solution)/shard_map/pack/pallas_call | solution.py:469
  2.3 17.8 %all_to_all.10.recv_ref = f32[32,16,128]{2,1,0:T(8,128)} all-to-all(f32[32,16,128]{2,1,0:T(8,128)} %pack.1), channel_id=1, replica_groups=mesh['gx'=4,'yz'=8] {'gx','yz'}, dimensions={0} | all-to-all | bytes 524288 | tf_op jit(solution)/shard_map/all_to_all | solution.py:477
  20.1 26.9 %sweep.1 = f32[32,4,128]{2,1,0:T(4,128)} custom-call(f32[32,16,128]{2,1,0:T(8,128)} %all_to_all.10.recv_ref, f32[112,128]{1,0:T(8,128)} %pair_ref.1, f32[128,128]{1,0:T(8,128)} %mix_ref.1, f32[1,128]{1,0:T(1,128)} %bitcast.8, f32[1,128]{1,0:T(1,128)} %bitcast.9), custom_call_target="tpu_custom_call" | custom-call | tf_op jit(solution)/shard_map/sweep/pallas_call | solution.py:480
  47.0 10.8 %all_to_all.11 = f32[32,4,128]{2,1,0:T(4,128)} all-to-all(f32[32,4,128]{2,1,0:T(4,128)} %sweep.1), channel_id=1, replica_groups=mesh['gx'=4,'yz'=8] {'gx','yz'}, dimensions={0} | all-to-all | bytes 131072 | tf_op jit(solution)/shard_map/all_to_all | solution.py:498
  57.8 1.5 %unpack.1 = (f32[48,128]{1,0:T(8,128)}, f32[48,128]{1,0:T(8,128)}) custom-call(f32[128,128]{1,0:T(8,128)} %bitcast.6), custom_call_target="tpu_custom_call" | custom-call | tf_op jit(solution)/shard_map/unpack/pallas_call | solution.py:502

commit v3 on v2

--- a/solution.py
+++ b/solution.py
@@ -128,46 +128,28 @@
     return sn, cosine, jnp.where(small, sine, sn / jnp.where(small, 1.0, v))
 
 
-def pack_kernel(n, sz, rep, half, halo, x_ref, out_ref, ext):
-    rows, cz = x_ref.shape
-    x = jnp.concatenate([x_ref[...], jnp.zeros((LANES - rows, cz), jnp.float32)], 0)
-    cells = x.T
-    ext[pl.ds(0, cz), :] = cells
-    ext[pl.ds(cz, half), :] = cells[:half]
-    upper = pltpu.roll(ext[pl.ds(half, cz), :], LANES // 2, axis=1)
-    lane = lax.broadcasted_iota(jnp.int32, (cz, LANES), 1)
-    both = jnp.where(lane < LANES // 2, cells, upper)
-    ext[pl.ds(half, cz), :] = both
-    ext[pl.ds(0, half), :] = both[cz - half :]
-
-    def send(d, carry):
-        start = (d // rep) * sz - halo + half
-        out_ref[d] = ext[pl.ds(start, half), :]
-        return carry
-
-    lax.fori_loop(0, n, send, 0, unroll=8)
-
-
-def unpack_kernel(in_ref, spin_ref, field_ref):
-    x = in_ref[...].T
-    n = spin_ref.shape[0]
-    spin_ref[...] = x[:n]
-    field_ref[...] = x[n : 2 * n]
-
-
-def sweep_kernel(
-    gx, yz, bx, by, cz, sz, rep, half, halo,
-    recv_ref, pair_ref, mix_ref, bias_ref, outw_ref,
-    out_ref,
-    spin, spin2, ver, cosv, grad, w1, w2, hidden,
+def runs_of(window, depth):
+    runs = []
+    for slot in range(8):
+        f, end = slot * depth, min((slot + 1) * depth, 3 * window)
+        while f < end:
+            c, z = divmod(f, window)
+            length = min(end - f, window - z)
+            runs.append((slot, f - slot * depth, length, c, z))
+            f += length
+    return runs
+
+
+def reach_below(z0, cz):
+    return jnp.where((z0 - 1 - cz // 2 + cz) % cz < REACH, REACH, REACH - 2)
+
+
+def pack_kernel(
+    n, sz, rep, window, depth,
+    x_ref, pair_ref, mix_ref, bias_ref, outw_ref,
+    out_ref, w1, w2,
+    ext, first, second,
 ):
-    pp = Plane(gx, yz, bx, by)
-    nt, cells = pp.nt, pp.cells
-    rows = spin.shape[2]
-    stride = 2 * rows + 1
-    blk = LANES // cells
-    window = 2 * half
-
     parts = []
     for k in range(NB):
         part = pair_ref[pl.ds(k, 14, stride=NB), :]
@@ -179,32 +161,96 @@
     rest = shift - split(shift)[0].astype(jnp.float32)
     rest = rest - split(rest)[0].astype(jnp.float32)
     hi, lo = split(jnp.where(row == 14, shift, jnp.where(row == 15, rest, w)).T)
-    w1[...] = jnp.concatenate(
-        [jnp.concatenate([hi, hi], 1), jnp.concatenate([lo, lo], 1)], 0
-    )
-    degree = lax.broadcasted_iota(jnp.int32, w.shape, 0) // OP + 1
+    w1[...] = jnp.concatenate([jnp.concatenate([hi, hi], 1), jnp.concatenate([lo, lo], 1)], 0)
+    degree = row // OP + 1
     hi, lo = split(w * degree.astype(jnp.float32) * outw_ref[...])
-    w2[...] = jnp.concatenate(
-        [jnp.concatenate([hi, hi], 1), jnp.concatenate([lo, lo], 1)], 0
-    )
-
-    lane16 = lax.broadcasted_iota(jnp.int32, (half, LANES), 1) // cells
+    w2[...] = jnp.concatenate([jnp.concatenate([hi, hi], 1), jnp.concatenate([lo, lo], 1)], 0)
+
+    rows, cz = x_ref.shape
+    field = rows // 3
+    x = jnp.concatenate([x_ref[...], jnp.zeros((LANES - rows, cz), jnp.float32)], 0)
+    cells = x.T
+    ext[pl.ds(0, cz), :] = cells
+    ext[pl.ds(cz, cz), :] = cells
+    runs = runs_of(window, depth)
+    lane = lax.broadcasted_iota(jnp.int32, (cz, LANES), 1) // field
+    margin = 16
+    for buf, chosen in ((first, [r for r in runs if r[1] == 0]), (second, [r for r in runs if r[1] > 0])):
+        total = cells
+        for slot, r, _, c, z in chosen:
+            part = ext[pl.ds((z - r) % cz, cz), :]
+            turn = (slot - c) * field % LANES
+            total = jnp.where(lane == slot, pltpu.roll(part, turn, axis=1) if turn else part, total)
+        buf[pl.ds(margin, cz), :] = total
+        buf[pl.ds(0, margin), :] = total[cz - margin :]
+        buf[pl.ds(margin + cz, margin), :] = total[:margin]
+
+    late = [(slot, r) for slot, r, _, _, _ in runs if r > 0]
+    row2 = lax.broadcasted_iota(jnp.int32, (2, LANES), 0)
+    slot2 = lax.broadcasted_iota(jnp.int32, (2, LANES), 1) // field
+
+    def send(d, carry):
+        z0 = (d // rep) * sz
+        start = z0 - reach_below(z0, cz) + margin
+        for q in range(depth // 2):
+            piece = first[pl.ds(start + 2 * q, 2), :]
+            mask = None
+            for slot, r in late:
+                if r < 2 * q + 2:
+                    m = (slot2 == slot) & (row2 + 2 * q >= r)
+                    mask = m if mask is None else mask | m
+            if mask is not None:
+                piece = jnp.where(mask, second[pl.ds(start + 2 * q, 2), :], piece)
+            out_ref[d, q] = piece
+        return carry
+
+    lax.fori_loop(0, n, send, 0, unroll=8)
+
+
+def unpack_kernel(in_ref, spin_ref, field_ref):
+    x = in_ref[...].T
+    n = spin_ref.shape[0]
+    spin_ref[...] = x[:n]
+    field_ref[...] = x[n : 2 * n]
+
+
+def sweep_kernel(
+    gx, yz, bx, by, cz, sz, rep, window, depth,
+    recv_ref, w1, w2,
+    out_ref,
+    spin, spin2, ver, cosv, grad, hidden, bricks,
+):
+    pp = Plane(gx, yz, bx, by)
+    nt, cells = pp.nt, pp.cells
+    rows = spin.shape[2]
+    stride = 2 * rows + 1
+    blk = LANES // cells
+
+    lane16 = lax.broadcasted_iota(jnp.int32, (16, LANES), 1) // cells
+    runs = runs_of(window, depth)
+
+    def arrive(d, carry):
+        for q in range(depth // 2):
+            bricks[d, pl.ds(2 * q, 2), :] = recv_ref[d, q]
+        return carry
+
+    lax.fori_loop(0, gx * yz, arrive, 0, unroll=8)
 
     def gather(t, carry):
         moved = []
         for k in range(blk):
-            v = recv_ref[t * blk + k]
+            v = bricks[t * blk + k]
             moved.append(pltpu.roll(v, k * cells, axis=1) if k else v)
-        for ca in range(6):
-            for h in range(2):
-                j = ca + h * (LANES // 2 // cells)
-                u = moved[0]
-                for k in range(1, blk):
-                    u = jnp.where(lane16 == (j + k) % blk, moved[k], u)
-                if j:
-                    u = pltpu.roll(u, LANES - j * cells, axis=1)
-                spin[ca, t, pl.ds(PAD + h * half, half), :] = u
-                spin2[ca, t, pl.ds(PAD + h * half, half), :] = u
+        for j in range(16):
+            u = moved[0]
+            for k in range(1, blk):
+                u = jnp.where(lane16 == (j + k) % blk, moved[k], u)
+            if j:
+                u = pltpu.roll(u, LANES - j * cells, axis=1)
+            for slot, r, length, c, z in runs:
+                if slot == j // 2:
+                    spin[2 * c + j % 2, t, pl.ds(PAD + z, length), :] = u[r : r + length]
+                    spin2[2 * c + j % 2, t, pl.ds(PAD + z, length), :] = u[r : r + length]
         return carry
 
     if nt <= 2:
@@ -218,12 +264,13 @@
     me = lax.axis_index("gx") * yz + lax.axis_index("yz")
     z0 = (me // rep) * sz
     hz = cz // 2
-    zs = (z0 - halo + cz) % cz
+    below = reach_below(z0, cz)
+    zs = (z0 - below + cz) % cz
     first = ((zs + hz - 1) // hz) * hz
     inside = first - zs < window
     border = PAD + first - zs
     hi_above = first % cz == hz
-    own = PAD + halo
+    own = PAD + below
 
     def is_hi(row):
         z = row - PAD + zs
@@ -400,7 +447,7 @@
         lax.fori_loop(0, count, body, 0)
 
     def take(everything):
-        for i in range(window // 8):
+        for i in range((window + 7) // 8):
             r = PAD + 8 * i
             row = lax.broadcasted_iota(jnp.int32, (8, LANES), 0) + r
             sel = everything | jnp.logical_not(is_hi(row))
@@ -459,28 +506,36 @@
     n = gx * yz
     sz = max(1, cz // n)
     rep = n * sz // cz
-    half = -(-(sz + 2 * REACH) // 16) * 8
-    halo = (2 * half - sz) // 2
-    rows = 2 * half + 2 * PAD
+    window = sz + 2 * REACH - 2
+    depth = -(-3 * window // 16) * 2
+    rows = -(-window // 8) * 8 + 2 * PAD
     nt = n * bx * by // LANES
     brick = three * two * bx * by
     vmem = pl.BlockSpec(memory_space=pltpu.VMEM)
 
-    packed = pl.pallas_call(
-        functools.partial(pack_kernel, n, sz, rep, half, halo),
-        out_shape=jax.ShapeDtypeStruct((n, half, LANES), jnp.float32),
-        in_specs=[vmem],
-        out_specs=vmem,
-        scratch_shapes=[pltpu.VMEM((cz + 2 * half, LANES), jnp.float32)],
+    f32, bf16 = jnp.float32, jnp.bfloat16
+    packed, w1, w2 = pl.pallas_call(
+        functools.partial(pack_kernel, n, sz, rep, window, depth),
+        out_shape=[
+            jax.ShapeDtypeStruct((n, depth // 2, 2, LANES), f32),
+            jax.ShapeDtypeStruct((2 * LANES, 2 * LANES), bf16),
+            jax.ShapeDtypeStruct((2 * LANES, 2 * LANES), bf16),
+        ],
+        in_specs=[vmem] * 5,
+        out_specs=[vmem] * 3,
+        scratch_shapes=[
+            pltpu.VMEM((2 * cz, LANES), f32),
+            pltpu.VMEM((cz + 32, LANES), f32),
+            pltpu.VMEM((cz + 32, LANES), f32),
+        ],
         name="pack",
-    )(spin_vectors.reshape(brick, cz))
+    )(spin_vectors.reshape(brick, cz), pair_weight, mix_weight, mix_bias[None], out_weight[None])
     received = lax.all_to_all(packed, ("gx", "yz"), 0, 0, tiled=True)
 
-    f32, bf16 = jnp.float32, jnp.bfloat16
     result = pl.pallas_call(
-        functools.partial(sweep_kernel, gx, yz, bx, by, cz, sz, rep, half, halo),
+        functools.partial(sweep_kernel, gx, yz, bx, by, cz, sz, rep, window, depth),
         out_shape=jax.ShapeDtypeStruct((n, sz, LANES), f32),
-        in_specs=[vmem] * 5,
+        in_specs=[vmem] * 3,
         out_specs=vmem,
         scratch_shapes=[
             pltpu.VMEM((6, nt, rows, LANES), f32),
@@ -488,13 +543,12 @@
             pltpu.VMEM((5, 6, nt, rows, LANES), f32),
             pltpu.VMEM((nt, OP * (2 * rows + 1) + 7, LANES), f32),
             pltpu.VMEM((nt, OP * (2 * rows + 1) + 7, LANES), f32),
-            pltpu.VMEM((2 * LANES, 2 * LANES), bf16),
-            pltpu.VMEM((2 * LANES, 2 * LANES), bf16),
             pltpu.VMEM((2, LANES, 2 * (2 - nt % 2) * LANES), f32),
+            pltpu.VMEM((n, 16, LANES), f32),
         ],
-        compiler_params=pltpu.CompilerParams(vmem_limit_bytes=58 * 2**20),
+        compiler_params=pltpu.CompilerParams(vmem_limit_bytes=min(56, 8 + 4 * nt) * 2**20),
         name="sweep",
-    )(received, pair_weight, mix_weight, mix_bias[None], out_weight[None])
+    )(received, w1, w2)
     returned = lax.all_to_all(result, ("gx", "yz"), 0, 0, tiled=True)
     if rep > 1:
         returned = returned[::rep]

time: 59.7 us -> 56.2 us (0.941)
  blocking collectives: 28.6 us -> 26.2 us
  Pallas kernels: 30.1 us -> 29.1 us
    all_to_all x1, blocking collectives: 17.8 us -> 15.8 us  [per_device(): received = lax.all_to_all(packed, ('gx', 'yz'), 0, 0, tiled=True)]
    pallas_call x1, Pallas kernels: 26.9 us -> 25.4 us  [per_device(): pl.pallas_call(functools.partial(sweep_kernel, gx, yz, bx, by, cz, sz, re...]
where the time goes in v3:
time: 56.2 us; the launch traced here: 55.9 us
  Pallas kernels  29.1 us (52%)
  blocking collectives  26.2 us (47%)
  between operations  0.64 us (1%)
    pallas_call x1, Pallas kernels, per_device(): pl.pallas_call(functools.partial(sweep_kernel, gx, yz, bx, by, cz, sz, re...  25.4 us
    all_to_all x1, blocking collectives, per_device(): received = lax.all_to_all(packed, ('gx', 'yz'), 0, 0, tiled=True)  15.8 us
    all_to_all x1, blocking collectives, per_device(): returned = lax.all_to_all(result, ('gx', 'yz'), 0, 0, tiled=True)  10.4 us
    pallas_call x1, Pallas kernels, per_device(): pl.pallas_call(functools.partial(pack_kernel, n, sz, rep, window, depth),...  2.21 us
    pallas_call x1, Pallas kernels, per_device(): pl.pallas_call(unpack_kernel, out_shape=[jax.ShapeDtypeStruct((brick, cz)...  1.54 us

profile of v3, /device:TPU:0, one launch (start us, length us, event | category | flops | bytes accessed | tf_op | source)
XLA Modules:
  0.0 55.9 jit_solution(5364679843024952639)
XLA Ops:
  0.6 2.2 %pack.1 = (f32[32,5,2,128]{3,2,1,0:T(2,128)}, bf16[256,256]{1,0:T(8,128)(2,1)}, bf16[256,256]{1,0:T(8,128)(2,1)}) custom-call(f32[48,128]{1,0:T(8,128)} %bitcast.7, f32[112,128]{1,0:T(8,128)} %pair_ref.1, f32[128,128]{1,0:T(8,128)} %mix_ref.1, f32[1,128]{1,0:T(1,128)} %bitcast.8, f32[1,128]{1,0:T(1,128)} %bitcast.9), custom_call_target="tpu_custom_call" | custom-call | tf_op jit(solution)/shard_map/pack/pallas_call | solution.py:517
  2.8 0.0 copy-start
  2.8 0.0 copy-start.1
  2.8 15.8 %all_to_all.10.recv_ref = f32[32,5,2,128]{3,2,1,0:T(2,128)S(1)} all-to-all(f32[32,5,2,128]{3,2,1,0:T(2,128)} %get-tuple-element.7), channel_id=1, replica_groups=mesh['gx'=4,'yz'=8] {'gx','yz'}, dimensions={0} | all-to-all | bytes 327680 | tf_op jit(solution)/shard_map/all_to_all | solution.py:533
  18.6 0.0 copy-done
  18.6 0.0 copy-done.1
  18.6 25.4 %sweep.1 = f32[32,4,128]{2,1,0:T(4,128)S(1)} custom-call(f32[32,5,2,128]{3,2,1,0:T(2,128)S(1)} %all_to_all.10.recv_ref, bf16[256,256]{1,0:T(8,128)(2,1)S(1)} %copy-done, bf16[256,256]{1,0:T(8,128)(2,1)S(1)} %copy-done.1), custom_call_target="tpu_custom_call" | custom-call | tf_op jit(solution)/shard_map/sweep/pallas_call | solution.py:535
  44.0 10.4 %all_to_all.11 = f32[32,4,128]{2,1,0:T(4,128)} all-to-all(f32[32,4,128]{2,1,0:T(4,128)S(1)} %sweep.1), channel_id=1, replica_groups=mesh['gx'=4,'yz'=8] {'gx','yz'}, dimensions={0} | all-to-all | bytes 131072 | tf_op jit(solution)/shard_map/all_to_all | solution.py:552
  54.4 1.5 %unpack.1 = (f32[48,128]{1,0:T(8,128)}, f32[48,128]{1,0:T(8,128)}) custom-call(f32[128,128]{1,0:T(8,128)} %bitcast.6), custom_call_target="tpu_custom_call" | custom-call | tf_op jit(solution)/shard_map/unpack/pallas_call | solution.py:556
Async XLA Ops:
  2.8 15.8 %copy-start = (bf16[256,256]{1,0:T(8,128)(2,1)S(1)}, bf16[256,256]{1,0:T(8,128)(2,1)}, u32[]{:S(2)}) copy-start(bf16[256,256]{1,0:T(8,128)(2,1)} %get-tuple-element.8.w1) | copy-start | bytes 393220
  2.8 15.8 %copy-start.1 = (bf16[256,256]{1,0:T(8,128)(2,1)S(1)}, bf16[256,256]{1,0:T(8,128)(2,1)}, u32[]{:S(2)}) copy-start(bf16[256,256]{1,0:T(8,128)(2,1)} %get-tuple-element.9.w2) | copy-start | bytes 393220

commit v4 on v3

--- a/solution.py
+++ b/solution.py
@@ -288,6 +288,22 @@
         low, high = f_low - 2, f_high + 2
     ranges = ranges[::-1]
 
+    def by_twos(count, body):
+        if isinstance(count, int):
+            for i in range(count):
+                body(i, 0)
+            return
+
+        def two(i, carry):
+            body(2 * i, carry)
+            return body(2 * i + 1, carry)
+
+        lax.fori_loop(0, count // 2, two, 0)
+
+        @pl.when(count % 2 == 1)
+        def _():
+            body(count - 1, 0)
+
     def shifted_spins(start, count):
         def body(i, carry):
             r = start + 8 * i
@@ -301,7 +317,7 @@
                         ver[n - 1, ca, t, pl.ds(r, 8), :] = got[t]
             return carry
 
-        lax.fori_loop(0, count, body, 0)
+        by_twos(count, body)
 
     def neighbour(c, a, dx, dy, t, r):
         n = versions(a).index((dx, dy))
@@ -322,7 +338,7 @@
                         cosv[t, pl.ds(o * stride + a * rows + r, 8), :] = total
             return carry
 
-        lax.fori_loop(0, count, body, 0)
+        by_twos(count, body)
 
     tc = 2 if nt % 2 == 0 else 1
     chunks = nt // tc
@@ -386,15 +402,19 @@
 
         total = count * chunks
         done = 2
-        for many in (4, 2):
-            def body(i, first, many=many):
-                for k in range(many):
-                    one(first + i * many + k, k % 2)
-                return first
-
-            times = (total - done) // many
-            lax.fori_loop(0, times, body, done)
-            done = done + times * many
+        if isinstance(total, int) and total <= 8:
+            for i in range(done, total):
+                one(i, i % 2)
+        else:
+            for many in (16, 8, 4, 2):
+                def body(i, first, many=many):
+                    for k in range(many):
+                        one(first + i * many + k, k % 2)
+                    return first
+
+                times = (total - done) // many
+                lax.fori_loop(0, times, body, done)
+                done = done + times * many
         for k in range(2):
             combine(total - 2 + k, backward(activate(k)))
 
@@ -418,8 +438,11 @@
         def body(i, carry):
             r = start + 8 * i
             row = lax.broadcasted_iota(jnp.int32, (8, LANES), 0) + r
-            from_border = jnp.where(hi_above, row - border, border - 1 - row)
-            wanted = jnp.logical_not(only_border) | ((from_border >= 0) & (from_border < 2))
+            if only_border:
+                from_border = jnp.where(hi_above, row - border, border - 1 - row)
+                wanted = (from_border >= 0) & (from_border < 2)
+            else:
+                wanted = True
             h = field(r)
             for a in range(2):
                 for t in range(nt):
@@ -444,45 +467,45 @@
                         spin2[2 * c + a, t, pl.ds(r, 8), :] = jnp.where(mask, new, old)
             return carry
 
-        lax.fori_loop(0, count, body, 0)
+        by_twos(count, body)
 
     def take(everything):
         for i in range((window + 7) // 8):
             r = PAD + 8 * i
             row = lax.broadcasted_iota(jnp.int32, (8, LANES), 0) + r
-            sel = everything | jnp.logical_not(is_hi(row))
+            sel = True if everything is True else everything | jnp.logical_not(is_hi(row))
             for ca in range(6):
                 for t in range(nt):
                     place = (ca, t, pl.ds(r, 8), slice(None))
-                    spin[place] = jnp.where(sel, spin2[place], spin[place])
-
-    def phase(p, carry):
-        stage, fix = p // 2, p % 2 == 1
+                    spin[place] = spin2[place] if sel is True else jnp.where(sel, spin2[place], spin[place])
+
+    def stage_pair(stage, carry):
         f_low, f_high = ranges[0]
-        for s in range(1, 5):
-            lo_s, hi_s = ranges[s] if s < 4 else (own, own + sz)
-            f_low = jnp.where(stage == s, lo_s, f_low)
-            f_high = jnp.where(stage == s, hi_s, f_high)
+        for s in range(1, 4):
+            f_low = jnp.where(stage == s, ranges[s][0], f_low)
+            f_high = jnp.where(stage == s, ranges[s][1], f_high)
         n = f_high - f_low
-        last = stage == 4
         crosses = inside & (f_low < border) & (border < f_high)
-
-        @pl.when(jnp.logical_not(fix) | crosses)
+        shifted_spins(f_low - 2, (n + 11) // 8)
+        cosines(f_low - 1, (n + 9) // 8)
+        gradients(f_low - 1, (n + 3) // 2 * 2)
+        update(f_low, (n + 7) // 8, stage, False)
+        take(jnp.logical_not(crosses))
+
+        @pl.when(crosses)
         def _():
-            shifted_spins(jnp.where(fix, border - 4, f_low - 2), jnp.where(fix, 1, (n + 11) // 8))
-            cosines(jnp.where(fix, border - 4, f_low - 1), jnp.where(fix, 1, (n + 9) // 8))
-            gradients(jnp.where(fix, border - 1, f_low - 1), jnp.where(fix, 2, (n + 3) // 2 * 2))
-
-            @pl.when(jnp.logical_not(last))
-            def _():
-                update(
-                    jnp.where(fix, border - 4, f_low), jnp.where(fix, 1, (n + 7) // 8), stage, fix
-                )
-                take(fix | jnp.logical_not(crosses))
+            shifted_spins(border - 4, 1)
+            cosines(border - 4, 1)
+            gradients(border - 1, 2)
+            update(border - 4, 1, stage, True)
+            take(True)
 
         return carry
 
-    lax.fori_loop(0, 9, phase, 0)
+    lax.fori_loop(0, 4, stage_pair, 0)
+    shifted_spins(own - 2, (sz + 11) // 8)
+    cosines(own - 1, (sz + 9) // 8)
+    gradients(own - 1, (sz + 3) // 2 * 2)
 
     final = field(own)
     lane16s = lax.broadcasted_iota(jnp.int32, (8, LANES), 1) // cells

time: 56.2 us -> 53.5 us (0.952)
  Pallas kernels: 29.1 us -> 26.4 us
    pallas_call x1, Pallas kernels: 25.4 us -> 22.6 us  [per_device(): pl.pallas_call(functools.partial(sweep_kernel, gx, yz, bx, by, cz, sz, re...]
where the time goes in v4:
time: 53.5 us; the launch traced here: 53.2 us
  Pallas kernels  26.4 us (49%)
  blocking collectives  26.2 us (49%)
  between operations  0.64 us (1%)
    pallas_call x1, Pallas kernels, per_device(): pl.pallas_call(functools.partial(sweep_kernel, gx, yz, bx, by, cz, sz, re...  22.6 us
    all_to_all x1, blocking collectives, per_device(): received = lax.all_to_all(packed, ('gx', 'yz'), 0, 0, tiled=True)  15.8 us
    all_to_all x1, blocking collectives, per_device(): returned = lax.all_to_all(result, ('gx', 'yz'), 0, 0, tiled=True)  10.4 us
    pallas_call x1, Pallas kernels, per_device(): pl.pallas_call(functools.partial(pack_kernel, n, sz, rep, window, depth),...  2.21 us
    pallas_call x1, Pallas kernels, per_device(): pl.pallas_call(unpack_kernel, out_shape=[jax.ShapeDtypeStruct((brick, cz)...  1.54 us

profile of v4, /device:TPU:0, one launch (start us, length us, event | category | flops | bytes accessed | tf_op | source)
XLA Modules:
  0.0 53.2 jit_solution(10691963088609255237)
XLA Ops:
  0.6 2.2 %pack.1 = (f32[32,5,2,128]{3,2,1,0:T(2,128)}, bf16[256,256]{1,0:T(8,128)(2,1)}, bf16[256,256]{1,0:T(8,128)(2,1)}) custom-call(f32[48,128]{1,0:T(8,128)} %bitcast.7, f32[112,128]{1,0:T(8,128)} %pair_ref.1, f32[128,128]{1,0:T(8,128)} %mix_ref.1, f32[1,128]{1,0:T(1,128)} %bitcast.8, f32[1,128]{1,0:T(1,128)} %bitcast.9), custom_call_target="tpu_custom_call" | custom-call | tf_op jit(solution)/shard_map/pack/pallas_call | solution.py:540
  2.8 0.0 copy-start
  2.8 0.0 copy-start.1
  2.8 15.8 %all_to_all.10.recv_ref = f32[32,5,2,128]{3,2,1,0:T(2,128)S(1)} all-to-all(f32[32,5,2,128]{3,2,1,0:T(2,128)} %get-tuple-element.7), channel_id=1, replica_groups=mesh['gx'=4,'yz'=8] {'gx','yz'}, dimensions={0} | all-to-all | bytes 327680 | tf_op jit(solution)/shard_map/all_to_all | solution.py:556
  18.6 0.0 copy-done
  18.6 0.0 copy-done.1
  18.6 22.6 %sweep.1 = f32[32,4,128]{2,1,0:T(4,128)S(1)} custom-call(f32[32,5,2,128]{3,2,1,0:T(2,128)S(1)} %all_to_all.10.recv_ref, bf16[256,256]{1,0:T(8,128)(2,1)S(1)} %copy-done, bf16[256,256]{1,0:T(8,128)(2,1)S(1)} %copy-done.1), custom_call_target="tpu_custom_call" | custom-call | tf_op jit(solution)/shard_map/sweep/pallas_call | solution.py:558
  41.3 10.4 %all_to_all.11 = f32[32,4,128]{2,1,0:T(4,128)} all-to-all(f32[32,4,128]{2,1,0:T(4,128)S(1)} %sweep.1), channel_id=1, replica_groups=mesh['gx'=4,'yz'=8] {'gx','yz'}, dimensions={0} | all-to-all | bytes 131072 | tf_op jit(solution)/shard_map/all_to_all | solution.py:575
  51.7 1.5 %unpack.1 = (f32[48,128]{1,0:T(8,128)}, f32[48,128]{1,0:T(8,128)}) custom-call(f32[128,128]{1,0:T(8,128)} %bitcast.6), custom_call_target="tpu_custom_call" | custom-call | tf_op jit(solution)/shard_map/unpack/pallas_call | solution.py:579
Async XLA Ops:
  2.8 15.8 %copy-start = (bf16[256,256]{1,0:T(8,128)(2,1)S(1)}, bf16[256,256]{1,0:T(8,128)(2,1)}, u32[]{:S(2)}) copy-start(bf16[256,256]{1,0:T(8,128)(2,1)} %get-tuple-element.8.w1) | copy-start | bytes 393220
  2.8 15.8 %copy-start.1 = (bf16[256,256]{1,0:T(8,128)(2,1)S(1)}, bf16[256,256]{1,0:T(8,128)(2,1)}, u32[]{:S(2)}) copy-start(bf16[256,256]{1,0:T(8,128)(2,1)} %get-tuple-element.9.w2) | copy-start | bytes 393220

commit v5 on v4

--- a/solution.py
+++ b/solution.py
@@ -207,13 +207,6 @@
     lax.fori_loop(0, n, send, 0, unroll=8)
 
 
-def unpack_kernel(in_ref, spin_ref, field_ref):
-    x = in_ref[...].T
-    n = spin_ref.shape[0]
-    spin_ref[...] = x[:n]
-    field_ref[...] = x[n : 2 * n]
-
-
 def sweep_kernel(
     gx, yz, bx, by, cz, sz, rep, window, depth,
     recv_ref, w1, w2,
@@ -289,7 +282,7 @@
     ranges = ranges[::-1]
 
     def by_twos(count, body):
-        if isinstance(count, int):
+        if isinstance(count, int) and nt <= 2:
             for i in range(count):
                 body(i, 0)
             return
@@ -298,6 +291,9 @@
             body(2 * i, carry)
             return body(2 * i + 1, carry)
 
+        if nt > 2:
+            lax.fori_loop(0, count, body, 0)
+            return
         lax.fori_loop(0, count // 2, two, 0)
 
         @pl.when(count % 2 == 1)
@@ -406,7 +402,7 @@
             for i in range(done, total):
                 one(i, i % 2)
         else:
-            for many in (16, 8, 4, 2):
+            for many in (16, 8, 4, 2) if chunks == 1 else (2,):
                 def body(i, first, many=many):
                     for k in range(many):
                         one(first + i * many + k, k % 2)
@@ -576,13 +572,8 @@
     if rep > 1:
         returned = returned[::rep]
 
-    outs = pl.pallas_call(
-        unpack_kernel,
-        out_shape=[jax.ShapeDtypeStruct((brick, cz), f32)] * 2,
-        in_specs=[vmem],
-        out_specs=[vmem] * 2,
-        name="unpack",
-    )(returned.reshape(cz, LANES))
+    flat = returned.reshape(cz, LANES).T
+    outs = [flat[:brick], flat[brick : 2 * brick]]
     return tuple(x.reshape(three, two, bx, by, cz) for x in outs)
 
 

time: 53.5 us -> 53.3 us (level)
  Pallas kernels: 26.4 us -> 24.8 us
  local copies, waits for them, and re-layouts: 0.01 us -> 1.47 us
    pallas_call x1 -> x0, Pallas kernels: 1.54 us -> none  [per_device(): pl.pallas_call(unpack_kernel, out_shape=[jax.ShapeDtypeStruct((brick, cz)...]
    slice x0 -> x3, local copies, waits for them, and re-layouts: none -> 1.46 us  [per_device(): outs = [flat[:brick], flat[brick:2 * brick]]]
where the time goes in v5:
time: 53.3 us; the launch traced here: 53 us
  blocking collectives  26.1 us (49%)
  Pallas kernels  24.8 us (47%)
  local copies, waits for them, and re-layouts  1.47 us (3%)
  between operations  0.64 us (1%)
    pallas_call x1, Pallas kernels, per_device(): pl.pallas_call(functools.partial(sweep_kernel, gx, yz, bx, by, cz, sz, re...  22.6 us
    all_to_all x1, blocking collectives, per_device(): received = lax.all_to_all(packed, ('gx', 'yz'), 0, 0, tiled=True)  15.8 us
    all_to_all x1, blocking collectives, per_device(): returned = lax.all_to_all(result, ('gx', 'yz'), 0, 0, tiled=True)  10.3 us
    pallas_call x1, Pallas kernels, per_device(): pl.pallas_call(functools.partial(pack_kernel, n, sz, rep, window, depth),...  2.21 us
    slice x3, local copies, waits for them, and re-layouts, per_device(): outs = [flat[:brick], flat[brick:2 * brick]]  1.46 us

profile of v5, /device:TPU:0, one launch (start us, length us, event | category | flops | bytes accessed | tf_op | source)
XLA Modules:
  0.0 53.0 jit_solution(1936987856133246901)
XLA Ops:
  0.6 2.2 %pack.1 = (f32[32,5,2,128]{3,2,1,0:T(2,128)}, bf16[256,256]{1,0:T(8,128)(2,1)}, bf16[256,256]{1,0:T(8,128)(2,1)}) custom-call(f32[48,128]{1,0:T(8,128)} %bitcast.9, f32[112,128]{1,0:T(8,128)} %pair_ref.1, f32[128,128]{1,0:T(8,128)} %mix_ref.1, f32[1,128]{1,0:T(1,128)} %bitcast.12, f32[1,128]{1,0:T(1,128)} %bitcast.13), custom_call_target="tpu_custom_call" | custom-call | tf_op jit(solution)/shard_map/pack/pallas_call | solution.py:536
  2.8 0.0 copy-start
  2.8 0.0 copy-start.1
  2.8 15.8 %all_to_all.10.recv_ref = f32[32,5,2,128]{3,2,1,0:T(2,128)S(1)} all-to-all(f32[32,5,2,128]{3,2,1,0:T(2,128)} %get-tuple-element.5), channel_id=1, replica_groups=mesh['gx'=4,'yz'=8] {'gx','yz'}, dimensions={0} | all-to-all | bytes 327680 | tf_op jit(solution)/shard_map/all_to_all | solution.py:552
  18.6 0.0 copy-done
  18.6 0.0 copy-done.1
  18.6 22.6 %sweep.1 = f32[32,4,128]{2,1,0:T(4,128)S(1)} custom-call(f32[32,5,2,128]{3,2,1,0:T(2,128)S(1)} %all_to_all.10.recv_ref, bf16[256,256]{1,0:T(8,128)(2,1)S(1)} %copy-done, bf16[256,256]{1,0:T(8,128)(2,1)S(1)} %copy-done.1), custom_call_target="tpu_custom_call" | custom-call | tf_op jit(solution)/shard_map/sweep/pallas_call | solution.py:554
  41.3 10.3 %all_to_all.11 = f32[32,4,128]{2,1,0:T(4,128)S(1)} all-to-all(f32[32,4,128]{2,1,0:T(4,128)S(1)} %sweep.1), channel_id=1, replica_groups=mesh['gx'=4,'yz'=8] {'gx','yz'}, dimensions={0} | all-to-all | bytes 131072 | tf_op jit(solution)/shard_map/all_to_all | solution.py:571
  51.6 0.1 fusion
  51.7 0.7 %copy.8 = f32[48,128]{1,0:T(8,128)} copy(f32[48,128]{0,1:T(8,128)S(1)} %get-tuple-element.8) | data formatting | bytes 49152 | tf_op jit(solution)/shard_map/slice | solution.py:576
  52.4 0.7 %copy.7 = f32[48,128]{1,0:T(8,128)} copy(f32[48,128]{0,1:T(8,128)S(1)} %get-tuple-element.9) | data formatting | bytes 49152 | tf_op jit(solution)/shard_map/slice | solution.py:576
Async XLA Ops:
  2.8 15.8 %copy-start = (bf16[256,256]{1,0:T(8,128)(2,1)S(1)}, bf16[256,256]{1,0:T(8,128)(2,1)}, u32[]{:S(2)}) copy-start(bf16[256,256]{1,0:T(8,128)(2,1)} %get-tuple-element.6.w1) | copy-start | bytes 393220
  2.8 15.8 %copy-start.1 = (bf16[256,256]{1,0:T(8,128)(2,1)S(1)}, bf16[256,256]{1,0:T(8,128)(2,1)}, u32[]{:S(2)}) copy-start(bf16[256,256]{1,0:T(8,128)(2,1)} %get-tuple-element.7.w2) | copy-start | bytes 393220

commit v6 on v5

--- a/solution.py
+++ b/solution.py
@@ -40,21 +40,21 @@
         self.nl = gx * yz * bx * by
         self.nt = self.nl // LANES
         self.lane = lax.broadcasted_iota(jnp.int32, (rows, LANES), 1)
-        ring = yz * self.cells
-        self.within = LANES % ring == 0
-        if self.within:
-            xl, yl, brick = self.at(0)
-            x_at = {0: self.lane, 1: jnp.where(xl == bx - 1, self.lane + ring - (bx - 1) * by, self.lane + by),
-                    -1: jnp.where(xl == 0, self.lane - ring + (bx - 1) * by, self.lane - by)}
-            hop = self.cells - (by - 1)
-            y_at = {0: 0, 1: jnp.where(yl < by - 1, 1, jnp.where(brick < yz - 1, hop, hop - ring)),
-                    -1: jnp.where(yl > 0, -1, jnp.where(brick > 0, -hop, ring - hop))}
-            self.source = {
-                (dx, dy): (x_at[dx] + y_at[dy] + LANES) % LANES for dx in (-1, 0, 1) for dy in (-1, 0, 1)
-            }
-            self.from_next = {1: (self.lane < ring) & (xl == 0), -1: (self.lane >= LANES - ring) & (xl == bx - 1)}
+        self.halves = self.nt == 2 and by == 2
+        if self.halves:
+            bricks = gx * yz // 2
+            x_in = self.lane // 2 % bx
+            brick = self.lane // self.cells + self.lane % 2 * bricks
+            self.source = {}
+            for dx in (-1, 0, 1):
+                for dy in (-1, 0, 1):
+                    x = (brick // yz * bx + x_in + dx + gx * bx) % (gx * bx)
+                    there = x // bx * yz + (brick % yz + dy + yz) % yz
+                    self.source[(dx, dy)] = there % bricks * self.cells + x % bx * 2 + there // bricks
 
     def at(self, t):
+        if self.halves:
+            return self.lane // 2 % self.bx, jnp.full_like(self.lane, t), None
         lane = self.lane + t * LANES
         return (lane // self.by) % self.bx, lane % self.by, (lane // self.cells) % self.yz
 
@@ -96,15 +96,30 @@
             out.append(jnp.where(yl == edge, far, inner[t]))
         return out
 
+    def step_half(self, v, dx, dy, t):
+        y = t + dy
+        if dx == 0 and y // 2 == 0:
+            return v[y % 2]
+        return jnp.take_along_axis(v[y % 2], self.source[(dx, y // 2)], axis=1, mode="promise_in_bounds")
+
+    def source_in(self, half, dx, dy):
+        if dy == 0:
+            return self.source[(dx, 0)]
+        first, second = self.source[(dx, dy // 2)], self.source[(dx, (1 + dy) // 2)]
+        return jnp.where(half == 0, first, second)
+
+    def swapped(self, v):
+        even = self.lane[: v[0].shape[0]] % 2 == 0
+        return [
+            jnp.where(even, v[0], pltpu.roll(v[1], 1, axis=1)),
+            jnp.where(even, pltpu.roll(v[0], LANES - 1, axis=1), v[1]),
+        ]
+
     def step(self, v, dx, dy):
         if not (dx or dy):
             return v
-        if self.within:
-            if dx and self.nt > 1:
-                swap = self.from_next[dx]
-                v = [jnp.where(swap, v[(t + dx) % self.nt], v[t]) for t in range(self.nt)]
-            where = self.source[(dx, dy)]
-            return [jnp.take_along_axis(x, where, axis=1, mode="promise_in_bounds") for x in v]
+        if self.halves:
+            return [self.step_half(v, dx, dy, t) for t in range(2)]
         return self.step_x(self.step_y(v, dy), dx)
 
 
@@ -251,6 +266,13 @@
             gather(t, 0)
     else:
         lax.fori_loop(0, nt, gather, 0)
+    if pp.halves:
+        for ca in range(6):
+            for i in range((window + 7) // 8):
+                at = [(ca, t, pl.ds(PAD + 8 * i, 8), slice(None)) for t in range(2)]
+                for t, v in enumerate(pp.swapped([spin[p] for p in at])):
+                    spin[at[t]] = v
+                    spin2[at[t]] = v
     for t in range(nt):
         cosv[t, pl.ds(14 * stride, 2 * stride), :] = jnp.ones((2 * stride, LANES), jnp.float32)
 
@@ -339,54 +361,80 @@
     tc = 2 if nt % 2 == 0 else 1
     chunks = nt // tc
 
+    def features(c):
+        c2 = c + c
+        kinds = [c, c2 * c - 1.0]
+        for _ in range(2, NB):
+            kinds.append(c2 * kinds[-1] - kinds[-2])
+        f_hi, f_lo = split(jnp.concatenate(kinds, 0))
+        return jnp.concatenate([f_hi, f_lo], 0)
+
+    def embedded(rhs):
+        z = jnp.dot(w1[...], rhs, preferred_element_type=jnp.float32)
+        return z[:LANES] + z[LANES:]
+
+    def activated(hid):
+        u = jnp.tanh(hid)
+        d_hi, d_lo = split(1.0 - u * u)
+        return jnp.concatenate([d_hi, d_lo], 0)
+
+    def backward(rhs):
+        y = jnp.dot(w2[...], rhs, preferred_element_type=jnp.float32)
+        return y[:LANES] + y[LANES:]
+
+    def slopes(c, y):
+        c2 = c + c
+        b1 = y[(NB - 1) * OP :]
+        b2 = None
+        for k in range(NB - 2, -1, -1):
+            new = y[k * OP : (k + 1) * OP] + c2 * b1
+            if b2 is not None:
+                new = new - b2
+            b1, b2 = new, b1
+        return b1
+
+    def bonds_at(t, a, r):
+        return t, pl.ds(a * rows + r, OP, stride=stride), slice(None)
+
+    def border_gradients(half):
+        near = [bonds_at(t, a, border - a) for a in range(2) for t in range(2)]
+        far = [bonds_at(half, a, border - 1 + a) for a in range(2)]
+        chunks_of = [near + far]
+        rhs = []
+        for part in chunks_of:
+            rhs.append(embedded(features(jnp.concatenate([cosv[p] for p in part], 1))))
+        for part, hid in zip(chunks_of, rhs):
+            c = jnp.concatenate([cosv[p] for p in part], 1)
+            g = slopes(c, backward(activated(hid)))
+            for n, p in enumerate(part):
+                grad[p] = g[:, n * LANES : (n + 1) * LANES]
+
     def gradients(start, count):
-        places = [(d, a, t) for d in range(1) for a in range(2) for t in range(tc)]
+        places = [(a, t) for a in range(2) for t in range(tc)]
 
         def place(i):
             if chunks == 1:
-                return start + 1 * i, 0
-            return start + 1 * (i // chunks), (i % chunks) * tc
+                return start + i, 0
+            return start + i // chunks, (i % chunks) * tc
 
         def cosine(i):
             r, t0 = place(i)
-            return jnp.concatenate(
-                [cosv[t0 + t, pl.ds(a * rows + r + d, OP, stride=stride), :] for d, a, t in places], 1
-            )
+            return jnp.concatenate([cosv[bonds_at(t0 + t, a, r)] for a, t in places], 1)
 
         def basis(i):
-            c = cosine(i)
-            c2 = c + c
-            kinds = [c, c2 * c - 1.0]
-            for _ in range(2, NB):
-                kinds.append(c2 * kinds[-1] - kinds[-2])
-            f_hi, f_lo = split(jnp.concatenate(kinds, 0))
-            return jnp.concatenate([f_hi, f_lo], 0)
+            return features(cosine(i))
 
         def forward(rhs, slot):
-            z = jnp.dot(w1[...], rhs, preferred_element_type=jnp.float32)
-            hidden[slot] = z[:LANES] + z[LANES:]
+            hidden[slot] = embedded(rhs)
 
         def activate(slot):
-            u = jnp.tanh(hidden[slot])
-            d_hi, d_lo = split(1.0 - u * u)
-            return jnp.concatenate([d_hi, d_lo], 0)
-
-        def backward(rhs):
-            y = jnp.dot(w2[...], rhs, preferred_element_type=jnp.float32)
-            return y[:LANES] + y[LANES:]
+            return activated(hidden[slot])
 
         def combine(i, y):
             r, t0 = place(i)
-            c2 = 2.0 * cosine(i)
-            b1 = y[(NB - 1) * OP :]
-            b2 = None
-            for k in range(NB - 2, -1, -1):
-                new = y[k * OP : (k + 1) * OP] + c2 * b1
-                if b2 is not None:
-                    new = new - b2
-                b1, b2 = new, b1
-            for n, (d, a, t) in enumerate(places):
-                grad[t0 + t, pl.ds(a * rows + r + d, OP, stride=stride), :] = b1[:, n * LANES : (n + 1) * LANES]
+            g = slopes(cosine(i), y)
+            for n, (a, t) in enumerate(places):
+                grad[bonds_at(t0 + t, a, r)] = g[:, n * LANES : (n + 1) * LANES]
 
         for k in range(2):
             forward(basis(k), k)
@@ -414,23 +462,46 @@
         for k in range(2):
             combine(total - 2 + k, backward(activate(k)))
 
-    def field(r):
+    def half_field(r, half, lanes):
+        out = []
+        for a in range(2):
+            total = [None] * 3
+            for o, (b, dx, dy, dz) in enumerate(bonds(a)):
+                m = mate_of(o)
+                theirs = grad[half if dy == 0 else 1 - half, pl.ds(m * stride + b * rows + r + dz, 8), :]
+                if dx or dy:
+                    theirs = jnp.take_along_axis(theirs, lanes[(dx, dy)], axis=1, mode="promise_in_bounds")
+                coeff = grad[half, pl.ds(o * stride + a * rows + r, 8), :] + theirs
+                for c in range(3):
+                    term = coeff * neighbour(c, b, dx, dy, half, r + dz)
+                    total[c] = term if total[c] is None else total[c] + term
+            out.append([-x for x in total])
+        return out
+
+    def field(r, tiles):
         out = []
         for a in range(2):
             total = [[None] * nt for _ in range(3)]
             for o, (b, dx, dy, dz) in enumerate(bonds(a)):
                 m = mate_of(o)
                 theirs = [grad[t, pl.ds(m * stride + b * rows + r + dz, 8), :] for t in range(nt)]
-                theirs = pp.step(theirs, dx, dy)
-                for t in range(nt):
+                if pp.halves:
+                    theirs = [pp.step_half(theirs, dx, dy, t) if t in tiles else None for t in range(nt)]
+                else:
+                    theirs = pp.step(theirs, dx, dy)
+                for t in tiles:
                     coeff = grad[t, pl.ds(o * stride + a * rows + r, 8), :] + theirs[t]
                     for c in range(3):
                         term = coeff * neighbour(c, b, dx, dy, t, r + dz)
                         total[c][t] = term if total[c][t] is None else total[c][t] + term
-            out.append([[-x for x in per] for per in total])
+            out.append([[None if x is None else -x for x in per] for per in total])
         return out
 
     def update(start, count, stage, only_border):
+        tiles = [stage % 2] if pp.halves else range(nt)
+        if pp.halves:
+            lanes = {(dx, dy): pp.source_in(tiles[0], dx, dy) for dx in (-1, 0, 1) for dy in (-1, 0, 1)}
+
         def body(i, carry):
             r = start + 8 * i
             row = lax.broadcasted_iota(jnp.int32, (8, LANES), 0) + r
@@ -439,9 +510,9 @@
                 wanted = (from_border >= 0) & (from_border < 2)
             else:
                 wanted = True
-            h = field(r)
+            h = half_field(r, tiles[0], lanes) if pp.halves else field(r, tiles)
             for a in range(2):
-                for t in range(nt):
+                for t in tiles:
                     xl, yl, _ = pp.at(t)
                     mask = (
                         ((xl >= bx // 2).astype(jnp.int32) == stage // 2)
@@ -449,7 +520,7 @@
                         & wanted
                     )
                     s = [spin[2 * c + a, t, pl.ds(r, 8), :] for c in range(3)]
-                    w = [TIME_STEP * h[a][c][t] for c in range(3)]
+                    w = [TIME_STEP * (h[a][c] if pp.halves else h[a][c][t]) for c in range(3)]
                     square = 0.25 * (w[0] * w[0] + w[1] * w[1] + w[2] * w[2])
                     sn, cs, hs = half_turn(square)
                     cosr = 1.0 - 2.0 * sn * sn
@@ -492,7 +563,10 @@
         def _():
             shifted_spins(border - 4, 1)
             cosines(border - 4, 1)
-            gradients(border - 1, 2)
+            if pp.halves:
+                border_gradients(stage % 2)
+            else:
+                gradients(border - 1, 2)
             update(border - 4, 1, stage, True)
             take(True)
 
@@ -503,13 +577,17 @@
     cosines(own - 1, (sz + 9) // 8)
     gradients(own - 1, (sz + 3) // 2 * 2)
 
-    final = field(own)
+    final = field(own, range(nt))
+    results = []
+    for j in range(12):
+        ca = j % 6
+        v = [spin[ca, t, pl.ds(own, 8), :] for t in range(nt)] if j < 6 else final[ca % 2][ca // 2]
+        results.append(pp.swapped(v) if pp.halves else v)
     lane16s = lax.broadcasted_iota(jnp.int32, (8, LANES), 1) // cells
     for t in range(nt):
         moved = []
         for j in range(12):
-            ca = j % 6
-            v = spin[ca, t, pl.ds(own, 8), :] if j < 6 else final[ca % 2][ca // 2][t]
+            v = results[j][t]
             moved.append(pltpu.roll(v, j * cells, axis=1) if j else v)
         for k in range(blk):
             u = moved[0]

time: 53.3 us -> 52.2 us (0.979)
  Pallas kernels: 24.8 us -> 23.6 us
    pallas_call x1, Pallas kernels: 22.6 us -> 21.4 us  [per_device(): pl.pallas_call(functools.partial(sweep_kernel, gx, yz, bx, by, cz, sz, re...]
where the time goes in v6:
time: 52.2 us; the launch traced here: 51.9 us
  blocking collectives  26.2 us (50%)
  Pallas kernels  23.6 us (45%)
  local copies, waits for them, and re-layouts  1.47 us (3%)
  between operations  0.64 us (1%)
    pallas_call x1, Pallas kernels, per_device(): pl.pallas_call(functools.partial(sweep_kernel, gx, yz, bx, by, cz, sz, re...  21.4 us
    all_to_all x1, blocking collectives, per_device(): received = lax.all_to_all(packed, ('gx', 'yz'), 0, 0, tiled=True)  15.8 us
    all_to_all x1, blocking collectives, per_device(): returned = lax.all_to_all(result, ('gx', 'yz'), 0, 0, tiled=True)  10.4 us
    pallas_call x1, Pallas kernels, per_device(): pl.pallas_call(functools.partial(pack_kernel, n, sz, rep, window, depth),...  2.21 us
    slice x3, local copies, waits for them, and re-layouts, per_device(): outs = [flat[:brick], flat[brick:2 * brick]]  1.46 us

profile of v6, /device:TPU:0, one launch (start us, length us, event | category | flops | bytes accessed | tf_op | source)
XLA Modules:
  0.0 51.9 jit_solution(10958482188968397272)
XLA Ops:
  0.6 2.2 %pack.1 = (f32[32,5,2,128]{3,2,1,0:T(2,128)}, bf16[256,256]{1,0:T(8,128)(2,1)}, bf16[256,256]{1,0:T(8,128)(2,1)}) custom-call(f32[48,128]{1,0:T(8,128)} %bitcast.9, f32[112,128]{1,0:T(8,128)} %pair_ref.1, f32[128,128]{1,0:T(8,128)} %mix_ref.1, f32[1,128]{1,0:T(1,128)} %bitcast.12, f32[1,128]{1,0:T(1,128)} %bitcast.13), custom_call_target="tpu_custom_call" | custom-call | tf_op jit(solution)/shard_map/pack/pallas_call | solution.py:614
  2.8 0.0 copy-start
  2.8 0.0 copy-start.1
  2.8 15.8 %all_to_all.10.recv_ref = f32[32,5,2,128]{3,2,1,0:T(2,128)S(1)} all-to-all(f32[32,5,2,128]{3,2,1,0:T(2,128)} %get-tuple-element.5), channel_id=1, replica_groups=mesh['gx'=4,'yz'=8] {'gx','yz'}, dimensions={0} | all-to-all | bytes 327680 | tf_op jit(solution)/shard_map/all_to_all | solution.py:630
  18.6 0.0 copy-done
  18.6 0.0 copy-done.1
  18.6 21.4 %sweep.1 = f32[32,4,128]{2,1,0:T(4,128)S(1)} custom-call(f32[32,5,2,128]{3,2,1,0:T(2,128)S(1)} %all_to_all.10.recv_ref, bf16[256,256]{1,0:T(8,128)(2,1)S(1)} %copy-done, bf16[256,256]{1,0:T(8,128)(2,1)S(1)} %copy-done.1), custom_call_target="tpu_custom_call" | custom-call | tf_op jit(solution)/shard_map/sweep/pallas_call | solution.py:632
  40.0 10.4 %all_to_all.11 = f32[32,4,128]{2,1,0:T(4,128)S(1)} all-to-all(f32[32,4,128]{2,1,0:T(4,128)S(1)} %sweep.1), channel_id=1, replica_groups=mesh['gx'=4,'yz'=8] {'gx','yz'}, dimensions={0} | all-to-all | bytes 131072 | tf_op jit(solution)/shard_map/all_to_all | solution.py:649
  50.5 0.1 fusion
  50.5 0.7 %copy.8 = f32[48,128]{1,0:T(8,128)} copy(f32[48,128]{0,1:T(8,128)S(1)} %get-tuple-element.8) | data formatting | bytes 49152 | tf_op jit(solution)/shard_map/slice | solution.py:654
  51.2 0.7 %copy.7 = f32[48,128]{1,0:T(8,128)} copy(f32[48,128]{0,1:T(8,128)S(1)} %get-tuple-element.9) | data formatting | bytes 49152 | tf_op jit(solution)/shard_map/slice | solution.py:654
Async XLA Ops:
  2.8 15.8 %copy-start = (bf16[256,256]{1,0:T(8,128)(2,1)S(1)}, bf16[256,256]{1,0:T(8,128)(2,1)}, u32[]{:S(2)}) copy-start(bf16[256,256]{1,0:T(8,128)(2,1)} %get-tuple-element.6.w1) | copy-start | bytes 393220
  2.8 15.8 %copy-start.1 = (bf16[256,256]{1,0:T(8,128)(2,1)S(1)}, bf16[256,256]{1,0:T(8,128)(2,1)}, u32[]{:S(2)}) copy-start(bf16[256,256]{1,0:T(8,128)(2,1)} %get-tuple-element.7.w2) | copy-start | bytes 393220

commit v7 on v6

--- a/solution.py
+++ b/solution.py
@@ -156,7 +156,10 @@
 
 
 def reach_below(z0, cz):
-    return jnp.where((z0 - 1 - cz // 2 + cz) % cz < REACH, REACH, REACH - 2)
+    close = (z0 - 1 - cz // 2 + cz) % cz < REACH
+    if isinstance(z0, int):
+        return REACH if close else REACH - 2
+    return jnp.where(close, REACH, REACH - 2)
 
 
 def pack_kernel(
@@ -219,7 +222,11 @@
             out_ref[d, q] = piece
         return carry
 
-    lax.fori_loop(0, n, send, 0, unroll=8)
+    if n <= 32:
+        for d in range(n):
+            send(d, 0)
+    else:
+        lax.fori_loop(0, n, send, 0, unroll=8)
 
 
 def sweep_kernel(
@@ -242,7 +249,11 @@
             bricks[d, pl.ds(2 * q, 2), :] = recv_ref[d, q]
         return carry
 
-    lax.fori_loop(0, gx * yz, arrive, 0, unroll=8)
+    if gx * yz <= 32:
+        for d in range(gx * yz):
+            arrive(d, 0)
+    else:
+        lax.fori_loop(0, gx * yz, arrive, 0, unroll=8)
 
     def gather(t, carry):
         moved = []
@@ -258,7 +269,8 @@
             for slot, r, length, c, z in runs:
                 if slot == j // 2:
                     spin[2 * c + j % 2, t, pl.ds(PAD + z, length), :] = u[r : r + length]
-                    spin2[2 * c + j % 2, t, pl.ds(PAD + z, length), :] = u[r : r + length]
+                    if not pp.halves:
+                        spin2[2 * c + j % 2, t, pl.ds(PAD + z, length), :] = u[r : r + length]
         return carry
 
     if nt <= 2:
@@ -450,7 +462,7 @@
             for i in range(done, total):
                 one(i, i % 2)
         else:
-            for many in (16, 8, 4, 2) if chunks == 1 else (2,):
+            for many in (20, 16, 8, 4, 2) if chunks == 1 else (2,):
                 def body(i, first, many=many):
                     for k in range(many):
                         one(first + i * many + k, k % 2)

time: 52.2 us -> 51.8 us (level)
  no operation moved by 1% of the time
where the time goes in v7:
time: 51.8 us; the launch traced here: 51.5 us
  blocking collectives  26.2 us (51%)
  Pallas kernels  23.2 us (45%)
  local copies, waits for them, and re-layouts  1.47 us (3%)
  between operations  0.64 us (1%)
    pallas_call x1, Pallas kernels, per_device(): pl.pallas_call(functools.partial(sweep_kernel, gx, yz, bx, by, cz, sz, re...  21.2 us
    all_to_all x1, blocking collectives, per_device(): received = lax.all_to_all(packed, ('gx', 'yz'), 0, 0, tiled=True)  15.8 us
    all_to_all x1, blocking collectives, per_device(): returned = lax.all_to_all(result, ('gx', 'yz'), 0, 0, tiled=True)  10.4 us
    pallas_call x1, Pallas kernels, per_device(): pl.pallas_call(functools.partial(pack_kernel, n, sz, rep, window, depth),...  2.03 us
    slice x3, local copies, waits for them, and re-layouts, per_device(): outs = [flat[:brick], flat[brick:2 * brick]]  1.46 us

profile of v7, /device:TPU:0, one launch (start us, length us, event | category | flops | bytes accessed | tf_op | source)
XLA Modules:
  0.0 51.5 jit_solution(14283873871209979076)
XLA Ops:
  0.6 2.0 %pack.1 = (f32[32,5,2,128]{3,2,1,0:T(2,128)}, bf16[256,256]{1,0:T(8,128)(2,1)}, bf16[256,256]{1,0:T(8,128)(2,1)}) custom-call(f32[48,128]{1,0:T(8,128)} %bitcast.9, f32[112,128]{1,0:T(8,128)} %pair_ref.1, f32[128,128]{1,0:T(8,128)} %mix_ref.1, f32[1,128]{1,0:T(1,128)} %bitcast.12, f32[1,128]{1,0:T(1,128)} %bitcast.13), custom_call_target="tpu_custom_call" | custom-call | tf_op jit(solution)/shard_map/pack/pallas_call | solution.py:626
  2.7 0.0 copy-start
  2.7 0.0 copy-start.1
  2.7 15.8 %all_to_all.10.recv_ref = f32[32,5,2,128]{3,2,1,0:T(2,128)S(1)} all-to-all(f32[32,5,2,128]{3,2,1,0:T(2,128)} %get-tuple-element.5), channel_id=1, replica_groups=mesh['gx'=4,'yz'=8] {'gx','yz'}, dimensions={0} | all-to-all | bytes 327680 | tf_op jit(solution)/shard_map/all_to_all | solution.py:642
  18.4 0.0 copy-done
  18.4 0.0 copy-done.1
  18.4 21.2 %sweep.1 = f32[32,4,128]{2,1,0:T(4,128)S(1)} custom-call(f32[32,5,2,128]{3,2,1,0:T(2,128)S(1)} %all_to_all.10.recv_ref, bf16[256,256]{1,0:T(8,128)(2,1)S(1)} %copy-done, bf16[256,256]{1,0:T(8,128)(2,1)S(1)} %copy-done.1), custom_call_target="tpu_custom_call" | custom-call | tf_op jit(solution)/shard_map/sweep/pallas_call | solution.py:644
  39.6 10.4 %all_to_all.11 = f32[32,4,128]{2,1,0:T(4,128)S(1)} all-to-all(f32[32,4,128]{2,1,0:T(4,128)S(1)} %sweep.1), channel_id=1, replica_groups=mesh['gx'=4,'yz'=8] {'gx','yz'}, dimensions={0} | all-to-all | bytes 131072 | tf_op jit(solution)/shard_map/all_to_all | solution.py:661
  50.1 0.1 fusion
  50.2 0.7 %copy.8 = f32[48,128]{1,0:T(8,128)} copy(f32[48,128]{0,1:T(8,128)S(1)} %get-tuple-element.8) | data formatting | bytes 49152 | tf_op jit(solution)/shard_map/slice | solution.py:666
  50.8 0.7 %copy.7 = f32[48,128]{1,0:T(8,128)} copy(f32[48,128]{0,1:T(8,128)S(1)} %get-tuple-element.9) | data formatting | bytes 49152 | tf_op jit(solution)/shard_map/slice | solution.py:666
Async XLA Ops:
  2.7 15.8 %copy-start = (bf16[256,256]{1,0:T(8,128)(2,1)S(1)}, bf16[256,256]{1,0:T(8,128)(2,1)}, u32[]{:S(2)}) copy-start(bf16[256,256]{1,0:T(8,128)(2,1)} %get-tuple-element.6.w1) | copy-start | bytes 393220
  2.7 15.8 %copy-start.1 = (bf16[256,256]{1,0:T(8,128)(2,1)S(1)}, bf16[256,256]{1,0:T(8,128)(2,1)}, u32[]{:S(2)}) copy-start(bf16[256,256]{1,0:T(8,128)(2,1)} %get-tuple-element.7.w2) | copy-start | bytes 393220

commit v8 on v7

--- a/solution.py
+++ b/solution.py
@@ -315,24 +315,30 @@
         low, high = f_low - 2, f_high + 2
     ranges = ranges[::-1]
 
-    def by_twos(count, body):
+    def by_threes(count, body):
         if isinstance(count, int) and nt <= 2:
             for i in range(count):
                 body(i, 0)
             return
 
-        def two(i, carry):
-            body(2 * i, carry)
-            return body(2 * i + 1, carry)
-
         if nt > 2:
             lax.fori_loop(0, count, body, 0)
             return
-        lax.fori_loop(0, count // 2, two, 0)
-
-        @pl.when(count % 2 == 1)
-        def _():
-            body(count - 1, 0)
+
+        def some(many):
+            def run(i, carry):
+                for k in range(many):
+                    body(3 * i + k, carry)
+                return carry
+
+            return run
+
+        lax.fori_loop(0, count // 3, some(3), 0)
+        for many in (1, 2):
+
+            @pl.when(count % 3 == many)
+            def _(many=many):
+                some(many)(count // 3, 0)
 
     def shifted_spins(start, count):
         def body(i, carry):
@@ -347,7 +353,7 @@
                         ver[n - 1, ca, t, pl.ds(r, 8), :] = got[t]
             return carry
 
-        by_twos(count, body)
+        by_threes(count, body)
 
     def neighbour(c, a, dx, dy, t, r):
         n = versions(a).index((dx, dy))
@@ -368,7 +374,7 @@
                         cosv[t, pl.ds(o * stride + a * rows + r, 8), :] = total
             return carry
 
-        by_twos(count, body)
+        by_threes(count, body)
 
     tc = 2 if nt % 2 == 0 else 1
     chunks = nt // tc
@@ -546,7 +552,7 @@
                         spin2[2 * c + a, t, pl.ds(r, 8), :] = jnp.where(mask, new, old)
             return carry
 
-        by_twos(count, body)
+        by_threes(count, body)
 
     def take(everything):
         for i in range((window + 7) // 8):

time: 51.8 us -> 51.5 us (level)
  no operation moved by 1% of the time
where the time goes in v8:
time: 51.5 us; the launch traced here: 51.3 us
  blocking collectives  26.1 us (51%)
  Pallas kernels  23.1 us (45%)
  local copies, waits for them, and re-layouts  1.47 us (3%)
  between operations  0.64 us (1%)
    pallas_call x1, Pallas kernels, per_device(): pl.pallas_call(functools.partial(sweep_kernel, gx, yz, bx, by, cz, sz, re...  21 us
    all_to_all x1, blocking collectives, per_device(): received = lax.all_to_all(packed, ('gx', 'yz'), 0, 0, tiled=True)  15.8 us
    all_to_all x1, blocking collectives, per_device(): returned = lax.all_to_all(result, ('gx', 'yz'), 0, 0, tiled=True)  10.3 us
    pallas_call x1, Pallas kernels, per_device(): pl.pallas_call(functools.partial(pack_kernel, n, sz, rep, window, depth),...  2.03 us
    slice x3, local copies, waits for them, and re-layouts, per_device(): outs = [flat[:brick], flat[brick:2 * brick]]  1.46 us

profile of v8, /device:TPU:0, one launch (start us, length us, event | category | flops | bytes accessed | tf_op | source)
XLA Modules:
  0.0 51.3 jit_solution(5357257854986276004)
XLA Ops:
  0.6 2.0 %pack.1 = (f32[32,5,2,128]{3,2,1,0:T(2,128)}, bf16[256,256]{1,0:T(8,128)(2,1)}, bf16[256,256]{1,0:T(8,128)(2,1)}) custom-call(f32[48,128]{1,0:T(8,128)} %bitcast.9, f32[112,128]{1,0:T(8,128)} %pair_ref.1, f32[128,128]{1,0:T(8,128)} %mix_ref.1, f32[1,128]{1,0:T(1,128)} %bitcast.12, f32[1,128]{1,0:T(1,128)} %bitcast.13), custom_call_target="tpu_custom_call" | custom-call | tf_op jit(solution)/shard_map/pack/pallas_call | solution.py:632
  2.7 0.0 copy-start
  2.7 0.0 copy-start.1
  2.7 15.8 %all_to_all.10.recv_ref = f32[32,5,2,128]{3,2,1,0:T(2,128)S(1)} all-to-all(f32[32,5,2,128]{3,2,1,0:T(2,128)} %get-tuple-element.5), channel_id=1, replica_groups=mesh['gx'=4,'yz'=8] {'gx','yz'}, dimensions={0} | all-to-all | bytes 327680 | tf_op jit(solution)/shard_map/all_to_all | solution.py:648
  18.4 0.0 copy-done
  18.4 0.0 copy-done.1
  18.4 21.0 %sweep.1 = f32[32,4,128]{2,1,0:T(4,128)S(1)} custom-call(f32[32,5,2,128]{3,2,1,0:T(2,128)S(1)} %all_to_all.10.recv_ref, bf16[256,256]{1,0:T(8,128)(2,1)S(1)} %copy-done, bf16[256,256]{1,0:T(8,128)(2,1)S(1)} %copy-done.1), custom_call_target="tpu_custom_call" | custom-call | tf_op jit(solution)/shard_map/sweep/pallas_call | solution.py:650
  39.5 10.3 %all_to_all.11 = f32[32,4,128]{2,1,0:T(4,128)S(1)} all-to-all(f32[32,4,128]{2,1,0:T(4,128)S(1)} %sweep.1), channel_id=1, replica_groups=mesh['gx'=4,'yz'=8] {'gx','yz'}, dimensions={0} | all-to-all | bytes 131072 | tf_op jit(solution)/shard_map/all_to_all | solution.py:667
  49.8 0.1 fusion
  49.9 0.7 %copy.8 = f32[48,128]{1,0:T(8,128)} copy(f32[48,128]{0,1:T(8,128)S(1)} %get-tuple-element.8) | data formatting | bytes 49152 | tf_op jit(solution)/shard_map/slice | solution.py:672
  50.6 0.7 %copy.7 = f32[48,128]{1,0:T(8,128)} copy(f32[48,128]{0,1:T(8,128)S(1)} %get-tuple-element.9) | data formatting | bytes 49152 | tf_op jit(solution)/shard_map/slice | solution.py:672
Async XLA Ops:
  2.7 15.8 %copy-start = (bf16[256,256]{1,0:T(8,128)(2,1)S(1)}, bf16[256,256]{1,0:T(8,128)(2,1)}, u32[]{:S(2)}) copy-start(bf16[256,256]{1,0:T(8,128)(2,1)} %get-tuple-element.6.w1) | copy-start | bytes 393220
  2.7 15.8 %copy-start.1 = (bf16[256,256]{1,0:T(8,128)(2,1)S(1)}, bf16[256,256]{1,0:T(8,128)(2,1)}, u32[]{:S(2)}) copy-start(bf16[256,256]{1,0:T(8,128)(2,1)} %get-tuple-element.7.w2) | copy-start | bytes 393220
